TPU v7x, 128 devices: a whole 4x4x4 slice. The times are simulated.
128 devices in a mesh: grp: 4 (over y), tile: 32 (over x, z, core).
Axes of the slice: x: 4, y: 4, z: 4, core: 2. Of those that a mesh axis runs over, the one named last changes fastest.
Arguments:
- inverse_factor: bfloat16 [128, 2560, 2560], P(('grp', 'tile')), as said below
- border: bfloat16 [128, 2560, 512], P(('grp', 'tile')), as said below
- border_blocks: int32 [128, 4], P(('grp', 'tile')), may hold values from 0 to 31, as said below
- border_count: int32 [128], P(('grp', 'tile')), may hold values from 1 to 4, as said below
- first_diag: float32 [4096], P('tile'), may hold values from 0.5 to 2
Outputs:
- panel: float32 [4096, 256], P('tile')
- reduced: float32 [4096, 4096], P('tile')
Inputs may be any that keep to these rules, and one draw needn't show every extreme that they name: `border_blocks`: the entries of a row are distinct first-section block numbers; only the first border_count entries of a row are live. `border_count`: some scenario has 4 live blocks and some has 1. `inverse_factor`: each matrix is lower triangular with a diagonal between 1 and 2. `border`: real entries, most of magnitude below 3 / sqrt(20480).
All inputs are finite; a program needn't handle non-finite values.
Results may differ from a plain program's by a relative error of at most 0.0003.
Values sent between devices are 32-bit elements; how exact they have to be, the bound alone decides.
A program may use at most 192 MiB of HBM per device.

v0:
```python
import jax
import jax.numpy as jnp
from jax import lax
from jax.sharding import PartitionSpec as P

BLK = 128
PANELS = 2


def broadcast(value, axis, root):
    mine = lax.axis_index(axis) == root
    return lax.psum(jnp.where(mine, value, jnp.zeros_like(value)), axis)


def on_device(inverse_factor, border, border_blocks, border_count, first_diag):
    tiles = lax.axis_size("tile")
    owner_index = lax.axis_index("tile")
    rows = first_diag.shape[0]
    first = rows * tiles
    nblk = first // BLK
    per = rows // BLK
    width = border.shape[2]
    maxb = border_blocks.shape[1]
    live = (jnp.arange(width) // BLK < border_count[0]).astype(jnp.bfloat16)
    coupled = jnp.dot(
        inverse_factor[0], border[0] * live[None, :], preferred_element_type=jnp.float32
    ).astype(jnp.bfloat16)
    gram = lax.dot_general(
        coupled, coupled, (((0,), (0,)), ((), ())), preferred_element_type=jnp.float32
    )
    blocks = border_blocks[0]
    idents = blocks.astype(jnp.float32)
    owned_ids = (owner_index * per + jnp.arange(per)).astype(jnp.float32)
    all_ids = jnp.arange(nblk).astype(jnp.float32)
    grams = lax.all_gather(gram[None], "tile", axis=0, tiled=True)
    their_ids = lax.all_gather(idents[None], "tile", axis=0, tiled=True)
    count = grams.shape[0]
    shaped = grams.reshape(count, maxb, BLK, maxb, BLK)
    row_pick = (their_ids[:, :, None] == owned_ids[None, None, :]).astype(jnp.float32)
    col_pick = (their_ids[:, :, None] == all_ids[None, None, :]).astype(jnp.float32)
    owned_rows = jnp.einsum("qip,qirjc->prqjc", row_pick, shaped, precision=lax.Precision.HIGHEST)
    placed = jnp.einsum("prqjc,qjb->prbc", owned_rows, col_pick, precision=lax.Precision.HIGHEST)
    schur_rows = placed
    schur_rows = lax.psum(schur_rows, "grp")
    diag_part = first_diag.reshape(per, BLK)
    own_block = (jnp.arange(nblk)[None, :] == owner_index * per + jnp.arange(per)[:, None]).astype(
        jnp.float32
    )
    diag_tiles = jnp.eye(BLK, dtype=jnp.float32)[None] * diag_part[:, :, None]
    schur_rows = schur_rows + own_block[:, None, :, None] * diag_tiles[:, :, None, :]
    schur_rows = schur_rows.reshape(rows, first)
    glob = owner_index * rows + jnp.arange(rows)
    columns = []
    for step in range(PANELS):
        root_dev = step // per
        local_row = step % per
        block = schur_rows[local_row * BLK : (local_row + 1) * BLK, step * BLK : (step + 1) * BLK]
        pivot_block = broadcast(block, "tile", root_dev)
        lower = jnp.linalg.cholesky(pivot_block)
        column = lax.linalg.triangular_solve(
            lower,
            schur_rows[:, step * BLK : (step + 1) * BLK],
            left_side=False,
            lower=True,
            transpose_a=True,
        )
        column = jnp.where((glob >= step * BLK)[:, None], column, 0.0)

        def update(piece, start, column=column):
            return jnp.dot(column, piece.T, precision=lax.Precision.HIGHEST)

        schur_rows = schur_rows - update(
            lax.all_gather(column, "tile", axis=0, tiled=True), jnp.int32(0)
        )
        columns.append(column)
    return (jnp.concatenate(columns, axis=1), schur_rows)


def solution(mesh):
    return jax.shard_map(
        on_device,
        mesh=mesh,
        in_specs=(
            P(("grp", "tile"), None, None),
            P(("grp", "tile"), None, None),
            P(("grp", "tile"), None),
            P(("grp", "tile")),
            P("tile"),
        ),
        out_specs=(P("tile", None), P("tile", None)),
        check_vma=False,
    )
```

profile of v0, /device:TPU:0, one launch (start us, length us, event | category | flops | bytes accessed | tf_op | source)
XLA Modules:
  0.0 660.4 jit_solution(18443786827166074424)
XLA Ops:
  7.9 27.5 %fusion.18 = f32[512,512]{1,0:T(8,128)} fusion(bf16[1,2560,2560]{2,1,0:T(8,128)(2,1)} %param.8, bf16[1,2560,512]{2,1,0:T(8,128)(2,1)} %param.9, bf16[512]{0:T(512)(128)(2,1)S(1)} %fusion.40), kind=kOutput, calls=%fused_computation.15 | convolution fusion | flops 8055685120 | bytes 16778240 | tf_op jit(solution)/shard_map/dot_general | solution.py:28
  35.5 23.1 %all-gather.1 = f32[32,1,4]{2,1,0:T(1,128)S(1)} all-gather(f32[1,1,4]{2,1,0:T(1,128)S(1)} %convert_bitcast_fusion), channel_id=1, replica_groups=mesh['grp'=4,'tile'=32] {'tile'}, dimensions={0}, use_global_device_ids=true | all-gather | bytes 528 | tf_op jit(solution)/shard_map/all_gather | solution.py:36
  58.8 93.1 %all-gather.10.cloned.1.call-done = f32[16384,512]{1,0:T(8,128)} async-done(((f32[512,512]{1,0:T(8,128)}), f32[16384,512]{1,0:T(8,128)}) %all-gather.10.cloned.1.call-update) | async-done | bytes 33554448 | tf_op jit(solution)/shard_map/all_gather | solution.py:35
  152.0 37.8 %reshape.110 = f32[32,4,128,4,128]{4,3,2,1,0:T(4,128)} reshape(f32[16384,512]{1,0:T(8,128)} %all-gather.10.cloned.1.call-done) | data formatting | bytes 67108864 | tf_op jit(solution)/shard_map/reshape | solution.py:38
  189.8 45.2 %fusion = f32[32,1,128,4,128]{4,1,3,2,0:T(1,128)S(1)} fusion(pred[32,4,1,1,1]{1,2,4,3,0:T(4,128)(4,1)S(1)} %copy.26, f32[32,4,128,4,128]{4,3,2,1,0:T(4,128)} %reshape.110), kind=kOutput, calls=%fused_computation | convolution fusion | flops 100663296 | bytes 41943168 | tf_op jit(solution)/shard_map/qip,qirjc->prqjc/dot_general | solution.py:41
  235.0 9.4 %fusion.12 = f32[1,128,32,128]{3,2,1,0:T(8,128)} fusion(f32[32,1,128,4,128]{4,1,3,2,0:T(1,128)S(1)} %fusion, f32[32,4]{0,1:T(4,128)S(1)} %bitcast.74, f32[32]{0:T(128)S(1)} %iota_convert_fusion), kind=kOutput, calls=%fused_computation.13 | convolution fusion | flops 805310464 | bytes 10486400 | tf_op jit(solution)/shard_map/prqjc,qjb->prbc/dot_general | solution.py:42
  245.2 57.3 %all-reduce.4.cloned.1.call-done = f32[1,128,32,128]{3,2,1,0:T(8,128)} async-done(((f32[1,128,32,128]{3,2,1,0:T(8,128)}), f32[1,128,32,128]{3,2,1,0:T(8,128)}) %all-reduce.4.cloned.1.call-update) | async-done | bytes 2097168 | tf_op jit(solution)/shard_map/psum | solution.py:44
  302.5 3.3 multiply_add_fusion
  305.8 2.0 copy.18
  308.8 95.0 %all-reduce.6.cloned.1.call-done = f32[128,128]{0,1:T(8,128)} async-done(((f32[128,128]{0,1:T(8,128)}), f32[128,128]{0,1:T(8,128)}) %all-reduce.6.cloned.1.call-update) | async-done | bytes 65552 | tf_op jit(solution)/shard_map/psum | solution.py:12
  403.8 0.9 copy.19
  405.6 11.7 %cholesky.44 = f32[128,128]{1,0:T(8,128)S(1)} custom-call(f32[128,128]{1,0:T(8,128)S(1)} %fusion.28), custom_call_target="Cholesky" | custom-call | tf_op jit(solution)/shard_map/jit(cholesky)/cholesky | solution.py:59
  418.6 9.8 %custom-call.6 = f32[1,128,128]{1,2,0:T(8,128)S(1)} custom-call(f32[1,128,128]{2,1,0:T(8,128)S(1)} %fusion.23), custom_call_target="InvertDiagBlocksLowerTriangular" | custom-call | tf_op jit(solution)/shard_map/triangular_solve/custom-call.0 | solution.py:60
  428.5 0.9 fusion.22
  429.5 43.9 %all-gather.6.cloned.1.call-done = f32[4096,128]{0,1:T(8,128)} async-done(((f32[128,128]{0,1:T(8,128)}), f32[4096,128]{0,1:T(8,128)}) %all-gather.6.cloned.1.call-update) | async-done | bytes 2097168 | tf_op jit(solution)/shard_map/all_gather | solution.py:73
  473.4 5.7 convolution_subtract_fusion.1
  480.0 94.5 %all-reduce.8.cloned.1.call-done = f32[128,128]{0,1:T(8,128)} async-done(((f32[128,128]{0,1:T(8,128)}), f32[128,128]{0,1:T(8,128)}) %all-reduce.8.cloned.1.call-update) | async-done | bytes 65552 | tf_op jit(solution)/shard_map/psum | solution.py:12
  574.5 0.9 copy.21
  576.3 11.7 %cholesky.55 = f32[128,128]{1,0:T(8,128)S(1)} custom-call(f32[128,128]{1,0:T(8,128)S(1)} %fusion.26), custom_call_target="Cholesky" | custom-call | tf_op jit(solution)/shard_map/jit(cholesky)/cholesky | solution.py:59
  589.3 9.8 %custom-call.7 = f32[1,128,128]{1,2,0:T(8,128)S(1)} custom-call(f32[1,128,128]{2,1,0:T(8,128)S(1)} %fusion.24), custom_call_target="InvertDiagBlocksLowerTriangular" | custom-call | tf_op jit(solution)/shard_map/triangular_solve/custom-call.0 | solution.py:60
  599.1 0.9 fusion.21
  601.7 42.3 %all-gather.8.cloned.1.call-done = f32[4096,128]{0,1:T(8,128)} async-done(((f32[128,128]{0,1:T(8,128)}), f32[4096,128]{0,1:T(8,128)}) %all-gather.8.cloned.1.call-update) | async-done | bytes 2097168 | tf_op jit(solution)/shard_map/all_gather | solution.py:73
  644.1 6.4 convolution_subtract_fusion
  650.4 2.9 copy.24
  (43 shorter events, 9.0 us)
Async XLA Ops:
  7.2 144.8 %all-gather.10.cloned.1.call-start = ((), (), s32[]{:S(2)}) async-start(), calls=%async_computation.5 | async-start | bytes 34603008 | tf_op jit(solution)/shard_map/all_gather | solution.py:35
  7.9 27.6 %copy-start.3 = (s32[1,4]{1,0:T(1,128)S(1)}, s32[1,4]{1,0:T(1,128)}, u32[]{:S(2)}) copy-start(s32[1,4]{1,0:T(1,128)} %param.10) | copy-start | bytes 52
  35.4 267.1 %all-reduce.4.cloned.1.call-start = ((), (), s32[]{:S(2)}) async-start(), calls=%async_computation | async-start | bytes 4194304 | tf_op jit(solution)/shard_map/psum | solution.py:44
  244.4 0.7 copy-start.2
  244.4 159.4 %all-reduce.6.cloned.1.call-start = ((), (), s32[]{:S(2)}) async-start(), calls=%async_computation.1 | async-start | bytes 131072 | tf_op jit(solution)/shard_map/psum | solution.py:12
  307.8 121.6 %copy-start = (f32[1,128,32,128]{1,3,2,0:T(8,128)}, f32[1,128,32,128]{1,3,2,0:T(8,128)S(1)}, u32[]{:S(2)}) copy-start(f32[1,128,32,128]{1,3,2,0:T(8,128)S(1)} %copy.18) | copy-start | bytes 6291460
  308.5 164.8 %all-gather.6.cloned.1.call-start = ((), (), s32[]{:S(2)}) async-start(), calls=%async_computation.2 | async-start | bytes 2162688 | tf_op jit(solution)/shard_map/all_gather | solution.py:73
  429.4 145.1 %all-reduce.8.cloned.1.call-start = ((), (), s32[]{:S(2)}) async-start(), calls=%async_computation.3 | async-start | bytes 131072 | tf_op jit(solution)/shard_map/psum | solution.py:12
  429.5 170.6 %copy-start.1 = (f32[128,128]{0,1:T(8,128)S(1)}, f32[128,128]{0,1:T(8,128)}, u32[]{:S(2)}) copy-start(f32[128,128]{0,1:T(8,128)} %fusion.22) | copy-start | bytes 196612
  479.7 164.4 %all-gather.8.cloned.1.call-start = ((), (), s32[]{:S(2)}) async-start(), calls=%async_computation.4 | async-start | bytes 2162688 | tf_op jit(solution)/shard_map/all_gather | solution.py:73
Sparse Core Ops, SparseCore 0:
  35.5 116.4 all-gather.9
  244.5 57.9 all-reduce.3
  308.6 95.0 all-reduce.5
  429.5 43.8 all-gather.5
  479.8 94.6 all-reduce.7
  600.2 43.8 all-gather.7
where the time goes:
time: 668 us; the launch traced here: 660 us
  waiting for transfers between devices  426 us (64%)
  matrix products  96 us (14%)
  other arithmetic  52.9 us (8%)
  local copies, waits for them, and re-layouts  46.2 us (7%)
  blocking collectives  23.1 us (3%)
  between operations  15.2 us (2%)
    psum x2, waiting for transfers between devices, broadcast(): return lax.psum(jnp.where(mine, value, jnp.zeros_like(value)), axis)  190 us
    all_gather x1, waiting for transfers between devices, on_device(): grams = lax.all_gather(gram[None], 'tile', axis=0, tiled=True)  93.1 us
    all_gather x2, waiting for transfers between devices, on_device(): lax.all_gather(column, 'tile', axis=0, tiled=True)  86.2 us
    psum x1, waiting for transfers between devices, on_device(): schur_rows = lax.psum(schur_rows, 'grp')  57.3 us
    dot_general x1, matrix products, on_device(): jnp.einsum('qip,qirjc->prqjc', row_pick, shaped, precision=lax.Precision....  45.2 us
    reshape x1, local copies, waits for them, and re-layouts, on_device(): shaped = grams.reshape(count, maxb, BLK, maxb, BLK)  37.8 us
    dot_general x1, matrix products, on_device(): lax.dot_general(coupled, coupled, (((0,), (0,)), ((), ())), preferred_ele...  27.5 us
    another operation x6, other arithmetic, on_device(): lower = jnp.linalg.cholesky(pivot_block)  24.8 us
  transfers between devices with their start and end apart: 6, of which 6 were waited for; matrix products, arithmetic and copies ran while one was open for 0% of the time, Pallas kernels for 0%

commit v1 on v0

v1 whole, which is shorter than its diff:
```python
import functools

import jax
import jax.numpy as jnp
from jax import lax
from jax.experimental import pallas as pl
from jax.experimental.pallas import tpu as pltpu
from jax.sharding import PartitionSpec as P

BLK = 128
MAXB = 4
NBLK = 32
ORDER = 2560
WIDTH = MAXB * BLK
DEV = 128
GRP = 4
TILE = 32
QUART = NBLK // GRP
STRIP = 512
STRIPS = ORDER // STRIP
PIECE1 = 24
PIECE2 = 16
PLACED = DEV * MAXB * MAXB
DEPTH = PLACED + BLK
MESH = pl.DeviceIdType.MESH
F32 = jnp.float32
BF16 = jnp.bfloat16
HIGHEST = lax.Precision.HIGHEST


def split(value):
    high = value.astype(BF16)
    return high, (value - high.astype(F32)).astype(BF16)


def dot(left, right, dims=((1,), (0,))):
    return lax.dot_general(left, right, (dims, ((), ())), preferred_element_type=F32)


def dot3(left, right, dims=((1,), (0,))):
    return dot(left[0], right[0], dims) + (dot(left[0], right[1], dims) + dot(left[1], right[0], dims))


def iota(shape, axis):
    return lax.broadcasted_iota(jnp.int32, shape, axis)


def peer_of(k, g, t):
    x, z, c = t // 8, (t // 2) % 4, t % 2
    dy, dx, dz, dc = k // 32, (k // 8) % 4, (k // 2) % 4, k % 2
    return (g + dy) % 4, ((x + dx) % 4) * 8 + ((z + dz) % 4) * 2 + (c + dc) % 2


class Ring:
    def __init__(self, view, own, me, up, down, send, recv, first):
        self.view, self.own, self.me = view, own, me
        self.up, self.down = up, down
        self.send, self.recv, self.first = send, recv, first

    def copy(self, src, dst, slot, device):
        made = pltpu.make_async_remote_copy(
            src, dst, self.send.at[self.first + slot], self.recv.at[self.first + slot],
            device_id=device, device_id_type=MESH)
        made.start()
        return made

    def start(self):
        me = self.me
        self.copies = [
            self.copy(self.own(0), self.view(me, 0), 0, self.up),
            self.copy(self.own(1), self.view(me, 1), 1, self.down),
            self.copy(self.own(1), self.view(me, 1), 2, self.up),
            self.copy(self.own(0), self.view(me, 0), 3, self.down),
        ]

    def middle(self):
        below, above = (self.me + 3) % 4, (self.me + 1) % 4
        self.copies[0].wait_recv()
        self.copies.append(self.copy(self.view(below, 0), self.view(below, 0), 4, self.up))
        self.copies[1].wait_recv()
        self.copies.append(self.copy(self.view(above, 1), self.view(above, 1), 5, self.down))

    def end(self):
        for made in self.copies[2:]:
            made.wait_recv()
        for made in self.copies:
            made.wait_send()


def factor_steps(a_ref, v_ref, first, last):
    sub = iota((8, BLK), 0)
    lane = iota((8, BLK), 1)

    def step(s, carry):
        base = pl.multiple_of(s * 8, 8)
        rows = a_ref[pl.ds(base, 8), :]
        inv_rows = v_ref[pl.ds(base, 8), :]
        cols = [
            jnp.take_along_axis(rows, jnp.full((8, BLK), base + p, jnp.int32), axis=1) for p in range(8)
        ]
        scale = jnp.zeros((8, BLK), F32)
        for p in range(8):
            recip = 1.0 / cols[p][p:p + 1, :]
            scale = jnp.where(sub == p, recip, scale)
            if p == 7:
                break
            by = jnp.where(sub > p, cols[p] * recip, 0.0)
            rows = rows - by * rows[p:p + 1, :]
            inv_rows = inv_rows - by * inv_rows[p:p + 1, :]
            for q in range(p + 1, 8):
                cols[q] = cols[q] - by * cols[q][p:p + 1, :]
        by = jnp.where(lane >= base + 8, rows * scale, 0.0).T
        a = a_ref[...]
        v = v_ref[...]
        for p in range(8):
            column = jnp.broadcast_to(by[:, p:p + 1], (BLK, BLK))
            a = a - column * rows[p:p + 1, :]
            v = v - column * inv_rows[p:p + 1, :]
        a_ref[...] = a
        v_ref[...] = v
        v_ref[pl.ds(base, 8), :] = inv_rows * jnp.sqrt(scale)
        return carry

    lax.fori_loop(first, last, step, 0)


def kernel(
    w_ref, b_ref, diag_ref, ids_ref, count_ref, panel_ref, reduced_ref,
    wbuf, bbuf, gram, send1, recv1, rhs, schur, send2, recv2, rows_all, cross, pivot, inverse,
    wsem, bsem, send_sem, recv_sem, own_sem, ring_send, ring_recv, core_send, core_recv,
):
    g = lax.axis_index("grp")
    t = lax.axis_index("tile")
    me = g * TILE + t
    x, z, c = t // 8, (t // 2) % 4, t % 2

    loads = []
    for i in range(STRIPS):
        rows = pl.ds(i * STRIP, STRIP)
        border = pltpu.make_async_copy(b_ref.at[0, rows], bbuf.at[rows], bsem.at[i])
        border.start()
        cols = pl.ds(0, (i + 1) * STRIP)
        factor = pltpu.make_async_copy(w_ref.at[0, rows, cols], wbuf.at[rows, cols], wsem.at[i])
        factor.start()
        loads.append((border, factor))

    barrier = pltpu.get_barrier_semaphore()

    def greet(k, carry):
        pl.semaphore_signal(barrier, inc=1, device_id=peer_of(k, g, t), device_id_type=MESH)
        return carry

    lax.fori_loop(1, DEV, greet, 0)

    live = iota((STRIP, WIDTH), 1) // BLK < count_ref[0]
    for i in range(STRIPS):
        rows = pl.ds(i * STRIP, STRIP)
        depth = pl.ds(0, (i + 1) * STRIP)
        loads[i][0].wait()
        bbuf[rows, :] = jnp.where(live, bbuf[rows, :], BF16(0))
        loads[i][1].wait()
        coupled = dot(wbuf[rows, depth], bbuf[depth, :]).astype(BF16)
        part = dot(coupled, coupled, ((0,), (0,)))
        if i == 0:
            gram[...] = part
        else:
            gram[...] += part

    for i in range(MAXB):
        for j in range(MAXB):
            send1[:, i * MAXB + j, :] = gram[i * BLK:(i + 1) * BLK, j * BLK:(j + 1) * BLK]
    lane = iota((BLK, BLK), 1)
    extra = jnp.where(lane == MAXB, jnp.broadcast_to(diag_ref[...], (BLK, BLK)).T, 0.0)
    for i in range(MAXB):
        extra = jnp.where(lane == i, ids_ref[0, i].astype(F32), extra)
    send1[:, MAXB * MAXB, :] = extra
    for i in range(MAXB * MAXB + 1, PIECE1):
        send1[:, i, :] = jnp.zeros((BLK, BLK), F32)

    pl.semaphore_wait(barrier, DEV - 1)

    def exchange(source, target, slot):
        def go(k, carry):
            g2, t2 = peer_of(k, g, t)
            pltpu.make_async_remote_copy(
                source.at[g2 * TILE + t2], target.at[me], send_sem.at[slot], recv_sem.at[slot],
                device_id=(g2, t2), device_id_type=MESH).start()
            return carry

        lax.fori_loop(1, DEV, go, 0)
        own = pltpu.make_async_copy(source.at[me], target.at[me], own_sem.at[slot])
        own.start()
        own.wait()
        every = pltpu.make_async_remote_copy(
            source.at[pl.ds(0, DEV - 1)], target.at[pl.ds(0, DEV - 1)], send_sem.at[slot],
            recv_sem.at[slot], device_id=(g, t), device_id_type=MESH)
        every.wait_recv()
        return every

    sent1 = exchange(send1, recv1, 0)

    extras = recv1[:, MAXB * MAXB, :]
    sel = iota((BLK, BLK), 0)
    pos = lane % (MAXB * MAXB)
    ids16 = extras.astype(BF16)
    at_lane = (sel % 8 == lane // (MAXB * MAXB)).astype(F32)
    gather = (iota((DEV // 8, DEV), 1) // 8 == iota((DEV // 8, DEV), 0)).astype(BF16)

    def along(which):
        spread = dot(ids16, (sel == which).astype(BF16)) * at_lane
        return dot(gather, spread.astype(BF16))

    keys = (along(pos // MAXB) * NBLK + along(pos % MAXB)).astype(jnp.int32)
    own_row = iota((1, BLK), 1)
    own_key = jnp.where(own_row < NBLK, own_row * (NBLK + 1), -1)
    diag = jnp.where((lane == me) & (sel < NBLK), jnp.broadcast_to(extras[:, MAXB:MAXB + 1], (BLK, BLK)), 0.0)
    high, low = split(recv1[:, 0:MAXB * MAXB, :].reshape(PLACED, BLK))
    rhs[0:PLACED, 0:BLK] = high
    rhs[0:PLACED, BLK:2 * BLK] = low
    high, low = split(diag)
    rhs[PLACED:DEPTH, 0:BLK] = high
    rhs[PLACED:DEPTH, BLK:2 * BLK] = low

    def place(m, carry):
        base = pl.multiple_of(m * 256, 256)
        target = iota((256, BLK), 0) + base
        hot = [
            jnp.where(target == keys[q:q + 1, :], F32(1), F32(0)).astype(BF16) for q in range(DEV // 8)
        ]
        hot.append(jnp.where(target == own_key, F32(1), F32(0)).astype(BF16))
        both = dot(jnp.concatenate(hot, axis=1), rhs[...])
        schur[pl.ds(base, 256), :] = both[:, 0:BLK] + both[:, BLK:2 * BLK]
        return carry

    lax.fori_loop(0, NBLK * NBLK // 256, place, 0)

    for h in range(GRP):
        for u in range(TILE):
            send2[h * TILE + u, 0:QUART, :] = schur[u * NBLK + h * QUART:u * NBLK + (h + 1) * QUART, :]
        some = pl.ds(h * TILE, TILE)
        for b in range(2):
            send2[some, QUART + b, :] = schur[b * NBLK:(b + 1) * NBLK, :]
            for e in range(2):
                send2[some, QUART + 2 + 2 * b + e, :] = jnp.broadcast_to(
                    schur[b * NBLK + e:b * NBLK + e + 1, :], (TILE, BLK))
            send2[some, QUART + 6 + b, :] = jnp.zeros((TILE, BLK), F32)
    sent2 = exchange(send2, recv2, 1)

    quarter = pltpu.make_async_copy(recv2.at[:, pl.ds(0, QUART)], rows_all.at[g], own_sem.at[2])
    quarter.start()
    for b in range(2):
        cross[b, x, z, c] = recv2[:, QUART + b, :]

    half = BLK // 2
    side = lambda s: pl.ds(s * half, half)
    at_x = lambda i: (g, i * 8 + z * 2 + c)
    at_z = lambda i: (g, x * 8 + i * 2 + c)
    up, down = (lambda i: (i + 1) % 4), (lambda i: (i + 3) % 4)
    ring_y = Ring(
        lambda i, s: rows_all.at[i, side(s)], lambda s: recv2.at[side(s), pl.ds(0, QUART)], g,
        (up(g), t), (down(g), t), ring_send, ring_recv, 0)

    def ring(view, position, at, first):
        return Ring(view, lambda s: view(position, s), position, at(up(position)), at(down(position)),
                    ring_send, ring_recv, first)

    ring_a1 = ring(lambda i, s: cross.at[0, i, z, c, side(s)], x, at_x, 6)
    ring_b1 = ring(lambda i, s: cross.at[1, x, i, c, side(s)], z, at_z, 12)
    ring_a2 = ring(lambda i, s: cross.at[0, :, i, c, side(s)], z, at_z, 18)
    ring_b2 = ring(lambda i, s: cross.at[1, i, :, c, side(s)], x, at_x, 24)

    ring_y.start()
    ring_a1.start()
    ring_b1.start()

    eye = jnp.where(sel == lane, F32(1), F32(0))
    pivot[...] = recv2[:, QUART + 2, :]
    inverse[0] = eye
    inverse[1] = eye
    factor_steps(pivot, inverse.at[0], 0, 4)
    ring_a1.middle()
    ring_b1.middle()
    factor_steps(pivot, inverse.at[0], 4, 8)
    ring_y.middle()
    ring_a1.end()
    ring_b1.end()
    ring_a2.start()
    ring_b2.start()
    factor_steps(pivot, inverse.at[0], 8, 16)
    ring_a2.middle()
    ring_b2.middle()
    below = lax.dot_general(
        recv2[:, QUART + 4, :], inverse[0], (((1,), (1,)), ((), ())), precision=HIGHEST,
        preferred_element_type=F32)
    pivot[...] = recv2[:, QUART + 5, :] - lax.dot_general(
        below, below, (((1,), (1,)), ((), ())), precision=HIGHEST, preferred_element_type=F32)
    factor_steps(pivot, inverse.at[1], 0, 8)
    ring_a2.end()
    ring_b2.end()
    other = (g, x * 8 + z * 2 + (1 - c))
    swaps = [
        pltpu.make_async_remote_copy(
            cross.at[b, :, :, c], cross.at[b, :, :, c], core_send.at[b], core_recv.at[b],
            device_id=other, device_id_type=MESH) for b in range(2)
    ]
    for swap in swaps:
        swap.start()
    factor_steps(pivot, inverse.at[1], 8, 16)
    first, second = inverse[0], inverse[1]
    mixed = -jnp.dot(
        second, jnp.dot(below, first, precision=HIGHEST, preferred_element_type=F32),
        precision=HIGHEST, preferred_element_type=F32)
    inv = split(jnp.concatenate(
        [jnp.concatenate([first, jnp.zeros((BLK, BLK), F32)], axis=1),
         jnp.concatenate([mixed, second], axis=1)], axis=0))

    quarter.wait()
    ring_y.end()
    own_cols = split(jnp.concatenate([rows_all[0, :, 0, :], rows_all[0, :, 1, :]], axis=1))
    panel = dot3(own_cols, inv, ((1,), (1,)))
    panel = jnp.where((t == 0) & (iota((BLK, 2 * BLK), 1) >= BLK), 0.0, panel)
    panel_ref[...] = panel
    panel = split(panel)
    for swap in swaps:
        swap.wait_recv()

    def update(n, carry):
        x2, z2 = n // 4, n % 4
        column = split(jnp.concatenate(
            [jnp.concatenate([cross[b, x2, z2, 0], cross[b, x2, z2, 1]], axis=1) for b in range(2)],
            axis=0))
        factor = dot3(inv, column)
        factor = jnp.where(
            (n == 0) & (iota((2 * BLK, 2 * BLK), 0) >= BLK) & (iota((2 * BLK, 2 * BLK), 1) < BLK),
            0.0, factor)
        change = dot3(panel, split(factor))
        h, q = n // 4, (n % 4) * 2
        before = jnp.concatenate([rows_all[h, :, q, :], rows_all[h, :, q + 1, :]], axis=1)
        reduced_ref[:, pl.ds(pl.multiple_of(n * 256, 256), 256)] = before - change
        return carry

    lax.fori_loop(0, NBLK // 2, update, 0)
    for swap in swaps:
        swap.wait_send()
    sent1.wait_send()
    sent2.wait_send()


def on_device(inverse_factor, border, border_blocks, border_count, first_diag):
    vmem = pl.BlockSpec(memory_space=pltpu.VMEM)
    smem = pl.BlockSpec(memory_space=pltpu.SMEM)
    hbm = pl.BlockSpec(memory_space=pl.ANY)
    dma = pltpu.SemaphoreType.DMA
    return pl.pallas_call(
        kernel,
        out_shape=(
            jax.ShapeDtypeStruct((BLK, 2 * BLK), F32),
            jax.ShapeDtypeStruct((BLK, NBLK * BLK), F32),
        ),
        in_specs=[hbm, hbm, vmem, smem, smem],
        out_specs=(vmem, vmem),
        scratch_shapes=[
            pltpu.VMEM((ORDER, ORDER), BF16),
            pltpu.VMEM((ORDER, WIDTH), BF16),
            pltpu.VMEM((WIDTH, WIDTH), F32),
            pltpu.VMEM((DEV, PIECE1, BLK), F32),
            pltpu.VMEM((DEV, PIECE1, BLK), F32),
            pltpu.VMEM((DEPTH, 2 * BLK), BF16),
            pltpu.VMEM((NBLK * NBLK, BLK), F32),
            pltpu.VMEM((DEV, PIECE2, BLK), F32),
            pltpu.VMEM((DEV, PIECE2, BLK), F32),
            pltpu.VMEM((GRP, BLK, QUART, BLK), F32),
            pltpu.VMEM((2, 4, 4, 2, BLK, BLK), F32),
            pltpu.VMEM((BLK, BLK), F32),
            pltpu.VMEM((2, BLK, BLK), F32),
            dma((STRIPS,)), dma((STRIPS,)), dma((2,)), dma((2,)), dma((3,)),
            dma((30,)), dma((30,)), dma((2,)), dma((2,)),
        ],
        compiler_params=pltpu.CompilerParams(
            collective_id=0, has_side_effects=True, vmem_limit_bytes=60 * 2**20),
        name="schur",
    )(inverse_factor, border, first_diag.reshape(1, BLK), border_blocks, border_count)


def solution(mesh):
    return jax.shard_map(
        on_device,
        mesh=mesh,
        in_specs=(
            P(("grp", "tile"), None, None),
            P(("grp", "tile"), None, None),
            P(("grp", "tile"), None),
            P(("grp", "tile")),
            P("tile"),
        ),
        out_specs=(P("tile", None), P("tile", None)),
        check_vma=False,
    )
```

time: 668 us -> 105 us (0.16); the launches traced: 660 us -> 105 us
  waiting for transfers between devices: 426 us -> 0 us
  Pallas kernels: 0 us -> 98.7 us
  matrix products: 96 us -> 0 us
  other arithmetic: 52.9 us -> 0 us
  local copies, waits for them, and re-layouts: 46.2 us -> 4.68 us
  blocking collectives: 23.1 us -> 0 us
  between operations: 15.2 us -> 1.29 us
    psum x3 -> x0, waiting for transfers between devices: 247 us -> none  [the longest x2 190 us: broadcast(): return lax.psum(jnp.where(mine, value, jnp.zeros_like(value)), axis)]
    all_gather x3 -> x0, waiting for transfers between devices: 179 us -> none  [the longest x1 93.1 us: on_device(): grams = lax.all_gather(gram[None], 'tile', axis=0, tiled=True)]
    pallas_call x0 -> x1, Pallas kernels: none -> 98.7 us  [on_device(): pl.pallas_call(kernel, out_shape=(jax.ShapeDtypeStruct((BLK, 2 * BLK), F3...]
    dot_general x5 -> x0, matrix products: 94.1 us -> none  [the longest x1 45.2 us: on_device(): jnp.einsum('qip,qirjc->prqjc', row_pick, shaped, precision=lax.Precision....]
    another operation x10 -> x0, other arithmetic: 45.7 us -> none  [the longest x6 24.8 us: on_device(): lower = jnp.linalg.cholesky(pivot_block)]
    reshape x1 -> x0, local copies, waits for them, and re-layouts: 37.8 us -> none  [on_device(): shaped = grams.reshape(count, maxb, BLK, maxb, BLK)]
    all_gather x1 -> x0, blocking collectives: 23.1 us -> none  [on_device(): their_ids = lax.all_gather(idents[None], 'tile', axis=0, tiled=True)]
  transfers between devices with their start and end apart: 6 -> 0, of which waited for: 6 -> 0; matrix products, arithmetic and copies ran while one was open for 0% -> 0% of each run, Pallas kernels for 0% -> 0%
where the time goes in v1:
time: 105 us
  Pallas kernels  98.7 us (94%)
  local copies, waits for them, and re-layouts  4.68 us (4%)
  between operations  1.29 us (1%)
    pallas_call x1, Pallas kernels, on_device(): pl.pallas_call(kernel, out_shape=(jax.ShapeDtypeStruct((BLK, 2 * BLK), F3...  98.7 us
    unnamed x2, local copies, waits for them, and re-layouts  4.68 us

profile of v1, /device:TPU:0, one launch (start us, length us, event | category | flops | bytes accessed | tf_op | source)
XLA Modules:
  0.0 104.6 jit_solution(10840029417125002060)
XLA Ops:
  1.3 98.7 %schur.1 = (f32[128,256]{1,0:T(8,128)}, f32[128,4096]{1,0:T(8,128)}) custom-call(bf16[1,2560,2560]{2,1,0:T(8,128)(2,1)} %w_ref.1, bf16[1,2560,512]{2,1,0:T(8,128)(2,1)} %b_ref.1, f32[1,128]{1,0:T(1,128)} %bitcast.1, s32[1,4]{1,0:T(1,128)} %ids_ref.1, s32[1]{0:T(128)S(6)} %copy.9.count_ref), custom_call_target="tpu_custom_call" | custom-call | tf_op jit(solution)/shard_map/schur/pallas_call | solution.py:354
  100.0 1.6 %copy.10 = f32[128,256]{1,0:T(8,128)} copy(f32[128,256]{1,0:T(8,128)} %get-tuple-element.4) | data formatting | bytes 262144
  101.5 3.1 %copy.11 = f32[128,4096]{1,0:T(8,128)} copy(f32[128,4096]{1,0:T(8,128)} %get-tuple-element.5) | data formatting | bytes 4194304

commit v2 on v1

--- a/solution.py
+++ b/solution.py
@@ -18,14 +18,16 @@
 QUART = NBLK // GRP
 STRIP = 512
 STRIPS = ORDER // STRIP
-PIECE1 = 24
+PAIRS = MAXB * (MAXB + 1) // 2
+PIECE1 = 16
+SENT1 = PAIRS + 1
 PIECE2 = 16
-PLACED = DEV * MAXB * MAXB
+SENT2 = QUART + 5
+PLACED = DEV * PIECE1
 DEPTH = PLACED + BLK
 MESH = pl.DeviceIdType.MESH
 F32 = jnp.float32
 BF16 = jnp.bfloat16
-HIGHEST = lax.Precision.HIGHEST
 
 
 def split(value):
@@ -37,8 +39,9 @@
     return lax.dot_general(left, right, (dims, ((), ())), preferred_element_type=F32)
 
 
-def dot3(left, right, dims=((1,), (0,))):
-    return dot(left[0], right[0], dims) + (dot(left[0], right[1], dims) + dot(left[1], right[0], dims))
+def dot_full(left, right, dims=((1,), (0,))):
+    return lax.dot_general(
+        left, right, (dims, ((), ())), precision=lax.Precision.HIGHEST, preferred_element_type=F32)
 
 
 def iota(shape, axis):
@@ -125,8 +128,8 @@
 
 
 def kernel(
-    w_ref, b_ref, diag_ref, ids_ref, count_ref, panel_ref, reduced_ref,
-    wbuf, bbuf, gram, send1, recv1, rhs, schur, send2, recv2, rows_all, cross, pivot, inverse,
+    w_ref, b_ref, diag_ref, ids_ref, count_ref, rows_all, cross, panel_ref, solved_ref,
+    wbuf, bbuf, gram, send1, recv1, rhs, schur, send2, recv2, mine, pivot, inverse,
     wsem, bsem, send_sem, recv_sem, own_sem, ring_send, ring_recv, core_send, core_recv,
 ):
     g = lax.axis_index("grp")
@@ -166,55 +169,64 @@
         else:
             gram[...] += part
 
+    p = 0
     for i in range(MAXB):
-        for j in range(MAXB):
-            send1[:, i * MAXB + j, :] = gram[i * BLK:(i + 1) * BLK, j * BLK:(j + 1) * BLK]
+        for j in range(i, MAXB):
+            block = gram[i * BLK:(i + 1) * BLK, j * BLK:(j + 1) * BLK]
+            if i < j:
+                ahead = jnp.full((BLK, BLK), ids_ref[0, i]) < jnp.full((BLK, BLK), ids_ref[0, j])
+                block = jnp.where(ahead, block, gram[j * BLK:(j + 1) * BLK, i * BLK:(i + 1) * BLK])
+            send1[:, p, :] = block
+            p += 1
     lane = iota((BLK, BLK), 1)
     extra = jnp.where(lane == MAXB, jnp.broadcast_to(diag_ref[...], (BLK, BLK)).T, 0.0)
     for i in range(MAXB):
         extra = jnp.where(lane == i, ids_ref[0, i].astype(F32), extra)
-    send1[:, MAXB * MAXB, :] = extra
-    for i in range(MAXB * MAXB + 1, PIECE1):
-        send1[:, i, :] = jnp.zeros((BLK, BLK), F32)
+    send1[:, PAIRS, :] = extra
 
     pl.semaphore_wait(barrier, DEV - 1)
 
-    def exchange(source, target, slot):
+    def exchange(source, target, rows, slot):
         def go(k, carry):
             g2, t2 = peer_of(k, g, t)
             pltpu.make_async_remote_copy(
-                source.at[g2 * TILE + t2], target.at[me], send_sem.at[slot], recv_sem.at[slot],
+                source.at[g2 * TILE + t2, rows], target.at[me, rows], send_sem.at[slot], recv_sem.at[slot],
                 device_id=(g2, t2), device_id_type=MESH).start()
             return carry
 
         lax.fori_loop(1, DEV, go, 0)
-        own = pltpu.make_async_copy(source.at[me], target.at[me], own_sem.at[slot])
+        own = pltpu.make_async_copy(source.at[me, rows], target.at[me, rows], own_sem.at[slot])
         own.start()
         own.wait()
         every = pltpu.make_async_remote_copy(
-            source.at[pl.ds(0, DEV - 1)], target.at[pl.ds(0, DEV - 1)], send_sem.at[slot],
+            source.at[pl.ds(0, DEV - 1), rows], target.at[pl.ds(0, DEV - 1), rows], send_sem.at[slot],
             recv_sem.at[slot], device_id=(g, t), device_id_type=MESH)
         every.wait_recv()
         return every
 
-    sent1 = exchange(send1, recv1, 0)
-
-    extras = recv1[:, MAXB * MAXB, :]
+    sent1 = exchange(send1, recv1, pl.ds(0, SENT1), 0)
+
+    extras = recv1[:, PAIRS, :]
     sel = iota((BLK, BLK), 0)
-    pos = lane % (MAXB * MAXB)
+    pos = lane % PIECE1
+    first = (pos >= 4).astype(jnp.int32) + (pos >= 7).astype(jnp.int32) + (pos >= 9).astype(jnp.int32)
+    second = jnp.where(first == 0, pos, jnp.where(first == 1, pos - 3, jnp.where(first == 2, pos - 5, pos - 6)))
     ids16 = extras.astype(BF16)
-    at_lane = (sel % 8 == lane // (MAXB * MAXB)).astype(F32)
+    at_lane = (sel % 8 == lane // PIECE1).astype(F32)
     gather = (iota((DEV // 8, DEV), 1) // 8 == iota((DEV // 8, DEV), 0)).astype(BF16)
 
     def along(which):
         spread = dot(ids16, (sel == which).astype(BF16)) * at_lane
         return dot(gather, spread.astype(BF16))
 
-    keys = (along(pos // MAXB) * NBLK + along(pos % MAXB)).astype(jnp.int32)
+    one, two = along(first), along(second)
+    keys = (jnp.minimum(one, two) * NBLK + jnp.maximum(one, two)).astype(jnp.int32)
+    keys = jnp.where(pos[0:DEV // 8, :] < PAIRS, keys, -1)
     own_row = iota((1, BLK), 1)
     own_key = jnp.where(own_row < NBLK, own_row * (NBLK + 1), -1)
     diag = jnp.where((lane == me) & (sel < NBLK), jnp.broadcast_to(extras[:, MAXB:MAXB + 1], (BLK, BLK)), 0.0)
-    high, low = split(recv1[:, 0:MAXB * MAXB, :].reshape(PLACED, BLK))
+    used = iota((DEV, PIECE1, BLK), 1) < PAIRS
+    high, low = split(jnp.where(used, recv1[...], 0.0).reshape(PLACED, BLK))
     rhs[0:PLACED, 0:BLK] = high
     rhs[0:PLACED, BLK:2 * BLK] = low
     high, low = split(diag)
@@ -223,7 +235,9 @@
 
     def place(m, carry):
         base = pl.multiple_of(m * 256, 256)
-        target = iota((256, BLK), 0) + base
+        place_row = iota((256, BLK), 0) + base
+        row, col = place_row // NBLK, place_row % NBLK
+        target = jnp.minimum(row, col) * NBLK + jnp.maximum(row, col)
         hot = [
             jnp.where(target == keys[q:q + 1, :], F32(1), F32(0)).astype(BF16) for q in range(DEV // 8)
         ]
@@ -240,16 +254,18 @@
         some = pl.ds(h * TILE, TILE)
         for b in range(2):
             send2[some, QUART + b, :] = schur[b * NBLK:(b + 1) * NBLK, :]
-            for e in range(2):
-                send2[some, QUART + 2 + 2 * b + e, :] = jnp.broadcast_to(
-                    schur[b * NBLK + e:b * NBLK + e + 1, :], (TILE, BLK))
-            send2[some, QUART + 6 + b, :] = jnp.zeros((TILE, BLK), F32)
-    sent2 = exchange(send2, recv2, 1)
-
-    quarter = pltpu.make_async_copy(recv2.at[:, pl.ds(0, QUART)], rows_all.at[g], own_sem.at[2])
-    quarter.start()
+        for e, r in enumerate((0, 1, NBLK + 1)):
+            send2[some, QUART + 2 + e, :] = jnp.broadcast_to(schur[r:r + 1, :], (TILE, BLK))
+    sent2 = exchange(send2, recv2, pl.ds(0, SENT2), 1)
+
+    mine[0] = recv2[:, QUART, :]
+    part = recv2[:, QUART + 1, :]
+    mine[1] = jnp.where(jnp.full((BLK, BLK), t) == 0, part.T, part)
+    owns = [pltpu.make_async_copy(recv2.at[:, pl.ds(0, QUART)], rows_all.at[g], own_sem.at[2])]
     for b in range(2):
-        cross[b, x, z, c] = recv2[:, QUART + b, :]
+        owns.append(pltpu.make_async_copy(mine.at[b], cross.at[b, x, z, c], own_sem.at[3 + b]))
+    for own in owns:
+        own.start()
 
     half = BLK // 2
     side = lambda s: pl.ds(s * half, half)
@@ -260,90 +276,88 @@
         lambda i, s: rows_all.at[i, side(s)], lambda s: recv2.at[side(s), pl.ds(0, QUART)], g,
         (up(g), t), (down(g), t), ring_send, ring_recv, 0)
 
-    def ring(view, position, at, first):
-        return Ring(view, lambda s: view(position, s), position, at(up(position)), at(down(position)),
-                    ring_send, ring_recv, first)
-
-    ring_a1 = ring(lambda i, s: cross.at[0, i, z, c, side(s)], x, at_x, 6)
-    ring_b1 = ring(lambda i, s: cross.at[1, x, i, c, side(s)], z, at_z, 12)
-    ring_a2 = ring(lambda i, s: cross.at[0, :, i, c, side(s)], z, at_z, 18)
-    ring_b2 = ring(lambda i, s: cross.at[1, i, :, c, side(s)], x, at_x, 24)
+    def ring(view, own, position, at, first):
+        return Ring(view, own, position, at(up(position)), at(down(position)), ring_send, ring_recv, first)
+
+    slab_a = lambda i, s: cross.at[0, :, i, c, side(s)]
+    slab_b = lambda i, s: cross.at[1, i, :, c, side(s)]
+    ring_a1 = ring(lambda i, s: cross.at[0, i, z, c, side(s)], lambda s: mine.at[0, side(s)], x, at_x, 6)
+    ring_b1 = ring(lambda i, s: cross.at[1, x, i, c, side(s)], lambda s: mine.at[1, side(s)], z, at_z, 12)
+    ring_a2 = ring(slab_a, lambda s: slab_a(z, s), z, at_z, 18)
+    ring_b2 = ring(slab_b, lambda s: slab_b(x, s), x, at_x, 24)
+    swaps = []
+
+    def swap(view):
+        made = pltpu.make_async_remote_copy(
+            view, view, core_send.at[len(swaps)], core_recv.at[len(swaps)],
+            device_id=(g, x * 8 + z * 2 + (1 - c)), device_id_type=MESH)
+        made.start()
+        swaps.append(made)
 
     ring_y.start()
     ring_a1.start()
     ring_b1.start()
-
     eye = jnp.where(sel == lane, F32(1), F32(0))
     pivot[...] = recv2[:, QUART + 2, :]
     inverse[0] = eye
     inverse[1] = eye
-    factor_steps(pivot, inverse.at[0], 0, 4)
+    factor_steps(pivot, inverse.at[0], 0, 3)
     ring_a1.middle()
     ring_b1.middle()
-    factor_steps(pivot, inverse.at[0], 4, 8)
-    ring_y.middle()
+    factor_steps(pivot, inverse.at[0], 3, 6)
+    for own in owns[1:]:
+        own.wait()
     ring_a1.end()
     ring_b1.end()
     ring_a2.start()
     ring_b2.start()
-    factor_steps(pivot, inverse.at[0], 8, 16)
+    swap(cross.at[0, :, z, c])
+    swap(cross.at[1, x, :, c])
+    ring_y.middle()
+    factor_steps(pivot, inverse.at[0], 6, 11)
     ring_a2.middle()
     ring_b2.middle()
-    below = lax.dot_general(
-        recv2[:, QUART + 4, :], inverse[0], (((1,), (1,)), ((), ())), precision=HIGHEST,
-        preferred_element_type=F32)
-    pivot[...] = recv2[:, QUART + 5, :] - lax.dot_general(
-        below, below, (((1,), (1,)), ((), ())), precision=HIGHEST, preferred_element_type=F32)
-    factor_steps(pivot, inverse.at[1], 0, 8)
+    factor_steps(pivot, inverse.at[0], 11, 16)
+    below = dot_full(recv2[:, QUART + 3, :], inverse[0], ((0,), (1,)))
+    pivot[...] = recv2[:, QUART + 4, :] - dot_full(below, below, ((1,), (1,)))
     ring_a2.end()
     ring_b2.end()
-    other = (g, x * 8 + z * 2 + (1 - c))
-    swaps = [
-        pltpu.make_async_remote_copy(
-            cross.at[b, :, :, c], cross.at[b, :, :, c], core_send.at[b], core_recv.at[b],
-            device_id=other, device_id_type=MESH) for b in range(2)
-    ]
-    for swap in swaps:
-        swap.start()
-    factor_steps(pivot, inverse.at[1], 8, 16)
+    for step in (1, 3, 2):
+        swap(cross.at[0, :, (z + step) % 4, c])
+        swap(cross.at[1, (x + step) % 4, :, c])
+    factor_steps(pivot, inverse.at[1], 0, 16)
     first, second = inverse[0], inverse[1]
-    mixed = -jnp.dot(
-        second, jnp.dot(below, first, precision=HIGHEST, preferred_element_type=F32),
-        precision=HIGHEST, preferred_element_type=F32)
-    inv = split(jnp.concatenate(
+    mixed = -dot_full(second, dot_full(below, first))
+    inv = jnp.concatenate(
         [jnp.concatenate([first, jnp.zeros((BLK, BLK), F32)], axis=1),
-         jnp.concatenate([mixed, second], axis=1)], axis=0))
-
-    quarter.wait()
+         jnp.concatenate([mixed, second], axis=1)], axis=0)
+    panel = dot_full(jnp.concatenate([mine[0], mine[1]], axis=0), inv, ((0,), (1,)))
+    panel_ref[...] = jnp.where(
+        (jnp.full((BLK, 2 * BLK), t) == 0) & (iota((BLK, 2 * BLK), 1) >= BLK), 0.0, panel)
+    solved_ref[...] = dot_full(panel, inv)
+
+    owns[0].wait()
     ring_y.end()
-    own_cols = split(jnp.concatenate([rows_all[0, :, 0, :], rows_all[0, :, 1, :]], axis=1))
-    panel = dot3(own_cols, inv, ((1,), (1,)))
-    panel = jnp.where((t == 0) & (iota((BLK, 2 * BLK), 1) >= BLK), 0.0, panel)
-    panel_ref[...] = panel
-    panel = split(panel)
-    for swap in swaps:
-        swap.wait_recv()
-
-    def update(n, carry):
-        x2, z2 = n // 4, n % 4
-        column = split(jnp.concatenate(
-            [jnp.concatenate([cross[b, x2, z2, 0], cross[b, x2, z2, 1]], axis=1) for b in range(2)],
-            axis=0))
-        factor = dot3(inv, column)
-        factor = jnp.where(
-            (n == 0) & (iota((2 * BLK, 2 * BLK), 0) >= BLK) & (iota((2 * BLK, 2 * BLK), 1) < BLK),
-            0.0, factor)
-        change = dot3(panel, split(factor))
-        h, q = n // 4, (n % 4) * 2
-        before = jnp.concatenate([rows_all[h, :, q, :], rows_all[h, :, q + 1, :]], axis=1)
-        reduced_ref[:, pl.ds(pl.multiple_of(n * 256, 256), 256)] = before - change
-        return carry
-
-    lax.fori_loop(0, NBLK // 2, update, 0)
-    for swap in swaps:
-        swap.wait_send()
+    for made in swaps:
+        made.wait()
     sent1.wait_send()
     sent2.wait_send()
+
+
+def update(rows_ref, cross_ref, panel_ref, solved_ref, panel_out, reduced_out):
+    t = lax.axis_index("tile")
+    n = pl.program_id(0)
+    panel_out[...] = panel_ref[...]
+    for q in range(0, QUART, 2):
+        before = []
+        for e in range(q, q + 2):
+            block = rows_ref[0, :, e, :]
+            behind = jnp.full((BLK, BLK), n * QUART + e) < jnp.full((BLK, BLK), t)
+            before.append(jnp.where(behind, block.T, block))
+        column = jnp.concatenate(
+            [jnp.concatenate([cross_ref[b, q], cross_ref[b, q + 1]], axis=1) for b in range(2)], axis=0)
+        reduced_out[:, q * BLK:(q + 2) * BLK] = jnp.concatenate(before, axis=1) - dot_full(
+            solved_ref[...], column)
 
 
 def on_device(inverse_factor, border, border_blocks, border_count, first_diag):
@@ -351,14 +365,16 @@
     smem = pl.BlockSpec(memory_space=pltpu.SMEM)
     hbm = pl.BlockSpec(memory_space=pl.ANY)
     dma = pltpu.SemaphoreType.DMA
-    return pl.pallas_call(
+    rows_all, cross, panel, solved = pl.pallas_call(
         kernel,
         out_shape=(
+            jax.ShapeDtypeStruct((GRP, BLK, QUART, BLK), F32),
+            jax.ShapeDtypeStruct((2, 4, 4, 2, BLK, BLK), F32),
             jax.ShapeDtypeStruct((BLK, 2 * BLK), F32),
-            jax.ShapeDtypeStruct((BLK, NBLK * BLK), F32),
+            jax.ShapeDtypeStruct((BLK, 2 * BLK), F32),
         ),
         in_specs=[hbm, hbm, vmem, smem, smem],
-        out_specs=(vmem, vmem),
+        out_specs=(hbm, hbm, vmem, vmem),
         scratch_shapes=[
             pltpu.VMEM((ORDER, ORDER), BF16),
             pltpu.VMEM((ORDER, WIDTH), BF16),
@@ -369,17 +385,33 @@
             pltpu.VMEM((NBLK * NBLK, BLK), F32),
             pltpu.VMEM((DEV, PIECE2, BLK), F32),
             pltpu.VMEM((DEV, PIECE2, BLK), F32),
-            pltpu.VMEM((GRP, BLK, QUART, BLK), F32),
-            pltpu.VMEM((2, 4, 4, 2, BLK, BLK), F32),
+            pltpu.VMEM((2, BLK, BLK), F32),
             pltpu.VMEM((BLK, BLK), F32),
             pltpu.VMEM((2, BLK, BLK), F32),
-            dma((STRIPS,)), dma((STRIPS,)), dma((2,)), dma((2,)), dma((3,)),
-            dma((30,)), dma((30,)), dma((2,)), dma((2,)),
+            dma((STRIPS,)), dma((STRIPS,)), dma((2,)), dma((2,)), dma((5,)),
+            dma((30,)), dma((30,)), dma((8,)), dma((8,)),
         ],
         compiler_params=pltpu.CompilerParams(
             collective_id=0, has_side_effects=True, vmem_limit_bytes=60 * 2**20),
         name="schur",
     )(inverse_factor, border, first_diag.reshape(1, BLK), border_blocks, border_count)
+    small = pl.BlockSpec((BLK, 2 * BLK), lambda n: (0, 0))
+    return pl.pallas_call(
+        update,
+        grid=(GRP,),
+        out_shape=(
+            jax.ShapeDtypeStruct((BLK, 2 * BLK), F32),
+            jax.ShapeDtypeStruct((BLK, NBLK * BLK), F32),
+        ),
+        in_specs=[
+            pl.BlockSpec((1, BLK, QUART, BLK), lambda n: (n, 0, 0, 0)),
+            pl.BlockSpec((2, QUART, BLK, BLK), lambda n: (0, n, 0, 0)),
+            small, small,
+        ],
+        out_specs=(small, pl.BlockSpec((BLK, QUART * BLK), lambda n: (0, n))),
+        compiler_params=pltpu.CompilerParams(vmem_limit_bytes=60 * 2**20),
+        name="update",
+    )(rows_all, cross.reshape(2, NBLK, BLK, BLK), panel, solved)
 
 
 def solution(mesh):

time: 105 us -> 86.1 us (0.82)
  Pallas kernels: 98.7 us -> 84.5 us
  local copies, waits for them, and re-layouts: 4.68 us -> 0 us
    pallas_call x1 -> x2, Pallas kernels: 98.7 us -> 84.5 us  [the longest x1 78.1 us: on_device(): pl.pallas_call(kernel, out_shape=(jax.ShapeDtypeStruct((GRP, BLK, QUART,...]
    unnamed x2 -> x0, local copies, waits for them, and re-layouts: 4.68 us -> none
where the time goes in v2:
time: 86.1 us; the launch traced here: 85.8 us
  Pallas kernels  84.5 us (98%)
  between operations  1.28 us (1%)
    pallas_call x1, Pallas kernels, on_device(): pl.pallas_call(kernel, out_shape=(jax.ShapeDtypeStruct((GRP, BLK, QUART,...  78.1 us
    pallas_call x1, Pallas kernels, on_device(): pl.pallas_call(update, grid=(GRP,), out_shape=(jax.ShapeDtypeStruct((BLK,...  6.47 us

profile of v2, /device:TPU:0, one launch (start us, length us, event | category | flops | bytes accessed | tf_op | source)
XLA Modules:
  0.0 85.8 jit_solution(12973879607286211631)
XLA Ops:
  1.3 78.1 %schur.1 = (f32[4,128,8,128]{3,2,1,0:T(8,128)}, f32[2,4,4,2,128,128]{5,4,3,2,1,0:T(8,128)}, f32[128,256]{1,0:T(8,128)}, f32[128,256]{1,0:T(8,128)}) custom-call(bf16[1,2560,2560]{2,1,0:T(8,128)(2,1)} %w_ref.1, bf16[1,2560,512]{2,1,0:T(8,128)(2,1)} %b_ref.1, f32[1,128]{1,0:T(1,128)} %bitcast.3, s32[1,4]{1,0:T(1,128)} %ids_ref.1, s32[1]{0:T(128)S(6)} %copy.7.count_ref), custom_call_target="tpu_custom_call" | custom-call | tf_op jit(solution)/shard_map/schur/pallas_call | solution.py:368
  79.4 6.5 %update.1 = (f32[128,256]{1,0:T(8,128)}, f32[128,4096]{1,0:T(8,128)}) custom-call(f32[4,128,8,128]{3,2,1,0:T(8,128)} %get-tuple-element.6.rows_ref, f32[2,32,128,128]{3,2,1,0:T(8,128)} %bitcast.2, f32[128,256]{1,0:T(8,128)} %get-tuple-element.8.panel_ref, f32[128,256]{1,0:T(8,128)} %get-tuple-element.9.solved_ref), custom_call_target="tpu_custom_call" | custom-call | tf_op jit(solution)/shard_map/update/pallas_call | solution.py:399

commit v3 on v2

--- a/solution.py
+++ b/solution.py
@@ -21,8 +21,7 @@
 PAIRS = MAXB * (MAXB + 1) // 2
 PIECE1 = 16
 SENT1 = PAIRS + 1
-PIECE2 = 16
-SENT2 = QUART + 5
+SENT2 = 5
 PLACED = DEV * PIECE1
 DEPTH = PLACED + BLK
 MESH = pl.DeviceIdType.MESH
@@ -83,8 +82,12 @@
         self.copies[1].wait_recv()
         self.copies.append(self.copy(self.view(above, 1), self.view(above, 1), 5, self.down))
 
+    def near(self):
+        for made in self.copies[2:4]:
+            made.wait_recv()
+
     def end(self):
-        for made in self.copies[2:]:
+        for made in self.copies[4:]:
             made.wait_recv()
         for made in self.copies:
             made.wait_send()
@@ -129,8 +132,8 @@
 
 def kernel(
     w_ref, b_ref, diag_ref, ids_ref, count_ref, rows_all, cross, panel_ref, solved_ref,
-    wbuf, bbuf, gram, send1, recv1, rhs, schur, send2, recv2, mine, pivot, inverse,
-    wsem, bsem, send_sem, recv_sem, own_sem, ring_send, ring_recv, core_send, core_recv,
+    wbuf, bbuf, gram, send1, recv1, rhs, send2, recv2, send3, recv3, small, mine, pivot, inverse,
+    wsem, bsem, send_sem, recv_sem, own_sem, ring_send, ring_recv, core_send, core_recv, greet_sem,
 ):
     g = lax.axis_index("grp")
     t = lax.axis_index("tile")
@@ -148,12 +151,16 @@
         loads.append((border, factor))
 
     barrier = pltpu.get_barrier_semaphore()
-
-    def greet(k, carry):
-        pl.semaphore_signal(barrier, inc=1, device_id=peer_of(k, g, t), device_id_type=MESH)
-        return carry
-
-    lax.fori_loop(1, DEV, greet, 0)
+    along_y = [((g + d) % 4, t) for d in (1, 2, 3)]
+    along_x = [(g, ((x + d) % 4) * 8 + z * 2 + c) for d in (1, 2, 3)]
+    along_z = [(g, x * 8 + ((z + d) % 4) * 2 + c) for d in (1, 2, 3)]
+    along_c = [(g, x * 8 + z * 2 + 1 - c)]
+
+    def greet(semaphore, peers):
+        for peer in peers:
+            pl.semaphore_signal(semaphore, inc=1, device_id=peer, device_id_type=MESH)
+
+    greet(barrier, along_y + along_x + along_z + along_c)
 
     live = iota((STRIP, WIDTH), 1) // BLK < count_ref[0]
     for i in range(STRIPS):
@@ -168,6 +175,15 @@
             gram[...] = part
         else:
             gram[...] += part
+        if i == 0:
+            pl.semaphore_wait(barrier, 10)
+            greet(greet_sem.at[0], along_x)
+        elif i == 1:
+            pl.semaphore_wait(greet_sem.at[0], 3)
+            greet(greet_sem.at[1], along_z)
+        elif i == 2:
+            pl.semaphore_wait(greet_sem.at[1], 3)
+            greet(greet_sem.at[2], along_c)
 
     p = 0
     for i in range(MAXB):
@@ -184,27 +200,33 @@
         extra = jnp.where(lane == i, ids_ref[0, i].astype(F32), extra)
     send1[:, PAIRS, :] = extra
 
-    pl.semaphore_wait(barrier, DEV - 1)
-
-    def exchange(source, target, rows, slot):
+    pl.semaphore_wait(greet_sem.at[2], 1)
+
+    def exchange(source, target, rows, count, slot):
+        here = t if count == TILE else me
+
         def go(k, carry):
             g2, t2 = peer_of(k, g, t)
+            there = t2 if count == TILE else g2 * TILE + t2
             pltpu.make_async_remote_copy(
-                source.at[g2 * TILE + t2, rows], target.at[me, rows], send_sem.at[slot], recv_sem.at[slot],
+                source.at[there, rows], target.at[here, rows], send_sem.at[slot], recv_sem.at[slot],
                 device_id=(g2, t2), device_id_type=MESH).start()
             return carry
 
-        lax.fori_loop(1, DEV, go, 0)
-        own = pltpu.make_async_copy(source.at[me, rows], target.at[me, rows], own_sem.at[slot])
+        lax.fori_loop(1, count, go, 0)
+        own = pltpu.make_async_copy(source.at[here, rows], target.at[here, rows], own_sem.at[slot])
         own.start()
-        own.wait()
         every = pltpu.make_async_remote_copy(
-            source.at[pl.ds(0, DEV - 1), rows], target.at[pl.ds(0, DEV - 1), rows], send_sem.at[slot],
+            source.at[pl.ds(0, count - 1), rows], target.at[pl.ds(0, count - 1), rows], send_sem.at[slot],
             recv_sem.at[slot], device_id=(g, t), device_id_type=MESH)
-        every.wait_recv()
-        return every
-
-    sent1 = exchange(send1, recv1, pl.ds(0, SENT1), 0)
+        return own, every
+
+    def received(exchanged):
+        exchanged[0].wait()
+        exchanged[1].wait_recv()
+
+    sent1 = exchange(send1, recv1, pl.ds(0, SENT1), DEV, 0)
+    received(sent1)
 
     extras = recv1[:, PAIRS, :]
     sel = iota((BLK, BLK), 0)
@@ -243,37 +265,40 @@
         ]
         hot.append(jnp.where(target == own_key, F32(1), F32(0)).astype(BF16))
         both = dot(jnp.concatenate(hot, axis=1), rhs[...])
-        schur[pl.ds(base, 256), :] = both[:, 0:BLK] + both[:, BLK:2 * BLK]
+        send3[pl.ds(m * 8, 8), :, :] = (both[:, 0:BLK] + both[:, BLK:2 * BLK]).reshape(8, NBLK, BLK)
         return carry
 
     lax.fori_loop(0, NBLK * NBLK // 256, place, 0)
 
-    for h in range(GRP):
-        for u in range(TILE):
-            send2[h * TILE + u, 0:QUART, :] = schur[u * NBLK + h * QUART:u * NBLK + (h + 1) * QUART, :]
-        some = pl.ds(h * TILE, TILE)
-        for b in range(2):
-            send2[some, QUART + b, :] = schur[b * NBLK:(b + 1) * NBLK, :]
-        for e, r in enumerate((0, 1, NBLK + 1)):
-            send2[some, QUART + 2 + e, :] = jnp.broadcast_to(schur[r:r + 1, :], (TILE, BLK))
-    sent2 = exchange(send2, recv2, pl.ds(0, SENT2), 1)
-
-    mine[0] = recv2[:, QUART, :]
-    part = recv2[:, QUART + 1, :]
-    mine[1] = jnp.where(jnp.full((BLK, BLK), t) == 0, part.T, part)
-    owns = [pltpu.make_async_copy(recv2.at[:, pl.ds(0, QUART)], rows_all.at[g], own_sem.at[2])]
     for b in range(2):
-        owns.append(pltpu.make_async_copy(mine.at[b], cross.at[b, x, z, c], own_sem.at[3 + b]))
-    for own in owns:
-        own.start()
-
-    half = BLK // 2
+        send2[:, b, :] = send3[b]
+    for e, (r, q) in enumerate(((0, 0), (0, 1), (1, 1))):
+        send2[:, 2 + e, :] = jnp.broadcast_to(send3[r, q:q + 1, :], (TILE, BLK))
+    sent2 = exchange(send2, recv2, pl.ds(0, SENT2), TILE, 1)
+    sent3 = exchange(send3, recv3, pl.ds(0, NBLK), TILE, 2)
+    received(sent2)
+
+    part = pl.ds(pl.multiple_of(g * TILE, TILE), TILE)
+    for e in range(5):
+        small[e, part, :] = recv2[:, e, :]
+    gathered = []
+    for slot, which in enumerate((pl.ds(2, 3), pl.ds(0, 2))):
+        for peer in (along_y[0], along_y[2], along_y[1]):
+            pltpu.make_async_remote_copy(
+                small.at[which, part], small.at[which, part], send_sem.at[3 + slot], recv_sem.at[3 + slot],
+                device_id=peer, device_id_type=MESH).start()
+        three = small.at[which, pl.ds(0, 3 * TILE)]
+        gathered.append(pltpu.make_async_remote_copy(
+            three, three, send_sem.at[3 + slot], recv_sem.at[3 + slot], device_id=(g, t), device_id_type=MESH))
+
+    half, some = BLK // 2, TILE // 2
     side = lambda s: pl.ds(s * half, half)
+    row_side = lambda s: pl.ds(s * some, some)
     at_x = lambda i: (g, i * 8 + z * 2 + c)
     at_z = lambda i: (g, x * 8 + i * 2 + c)
     up, down = (lambda i: (i + 1) % 4), (lambda i: (i + 3) % 4)
     ring_y = Ring(
-        lambda i, s: rows_all.at[i, side(s)], lambda s: recv2.at[side(s), pl.ds(0, QUART)], g,
+        lambda i, s: rows_all.at[i, row_side(s)], lambda s: recv3.at[row_side(s)], g,
         (up(g), t), (down(g), t), ring_send, ring_recv, 0)
 
     def ring(view, own, position, at, first):
@@ -294,38 +319,54 @@
         made.start()
         swaps.append(made)
 
-    ring_y.start()
+    eye = jnp.where(sel == lane, F32(1), F32(0))
+    inverse[0] = eye
+    inverse[1] = eye
+    gathered[0].wait_recv()
+    pivot[...] = small[2]
+    gathered[1].wait_recv()
+    mine[0] = small[0]
+    mine[1] = jnp.where(jnp.full((BLK, BLK), t) == 0, small[1].T, small[1])
     ring_a1.start()
     ring_b1.start()
-    eye = jnp.where(sel == lane, F32(1), F32(0))
-    pivot[...] = recv2[:, QUART + 2, :]
-    inverse[0] = eye
-    inverse[1] = eye
-    factor_steps(pivot, inverse.at[0], 0, 3)
+    owns = [pltpu.make_async_copy(recv3, rows_all.at[g], own_sem.at[3])]
+    for b in range(2):
+        owns.append(pltpu.make_async_copy(mine.at[b], cross.at[b, x, z, c], own_sem.at[4 + b]))
+        owns[-1].start()
+    factor_steps(pivot, inverse.at[0], 0, 4)
+    received(sent3)
+    ring_y.start()
+    owns[0].start()
     ring_a1.middle()
     ring_b1.middle()
-    factor_steps(pivot, inverse.at[0], 3, 6)
+    factor_steps(pivot, inverse.at[0], 4, 9)
     for own in owns[1:]:
         own.wait()
-    ring_a1.end()
-    ring_b1.end()
+    for made in (ring_a1, ring_b1):
+        made.near()
+        made.end()
     ring_a2.start()
     ring_b2.start()
     swap(cross.at[0, :, z, c])
     swap(cross.at[1, x, :, c])
+    factor_steps(pivot, inverse.at[0], 9, 16)
     ring_y.middle()
-    factor_steps(pivot, inverse.at[0], 6, 11)
+    below = dot_full(small[3], inverse[0], ((0,), (1,)))
+    pivot[...] = small[4] - dot_full(below, below, ((1,), (1,)))
     ring_a2.middle()
     ring_b2.middle()
-    factor_steps(pivot, inverse.at[0], 11, 16)
-    below = dot_full(recv2[:, QUART + 3, :], inverse[0], ((0,), (1,)))
-    pivot[...] = recv2[:, QUART + 4, :] - dot_full(below, below, ((1,), (1,)))
+    factor_steps(pivot, inverse.at[1], 0, 6)
+    ring_a2.near()
+    ring_b2.near()
+    for step in (1, 3):
+        swap(cross.at[0, :, (z + step) % 4, c])
+        swap(cross.at[1, (x + step) % 4, :, c])
+    factor_steps(pivot, inverse.at[1], 6, 11)
     ring_a2.end()
     ring_b2.end()
-    for step in (1, 3, 2):
-        swap(cross.at[0, :, (z + step) % 4, c])
-        swap(cross.at[1, (x + step) % 4, :, c])
-    factor_steps(pivot, inverse.at[1], 0, 16)
+    swap(cross.at[0, :, (z + 2) % 4, c])
+    swap(cross.at[1, (x + 2) % 4, :, c])
+    factor_steps(pivot, inverse.at[1], 11, 16)
     first, second = inverse[0], inverse[1]
     mixed = -dot_full(second, dot_full(below, first))
     inv = jnp.concatenate(
@@ -337,11 +378,12 @@
     solved_ref[...] = dot_full(panel, inv)
 
     owns[0].wait()
+    ring_y.near()
     ring_y.end()
     for made in swaps:
         made.wait()
-    sent1.wait_send()
-    sent2.wait_send()
+    for made in (sent1[1], sent2[1], sent3[1], *gathered):
+        made.wait_send()
 
 
 def update(rows_ref, cross_ref, panel_ref, solved_ref, panel_out, reduced_out):
@@ -351,7 +393,7 @@
     for q in range(0, QUART, 2):
         before = []
         for e in range(q, q + 2):
-            block = rows_ref[0, :, e, :]
+            block = rows_ref[:, :, e, :].reshape(BLK, BLK)
             behind = jnp.full((BLK, BLK), n * QUART + e) < jnp.full((BLK, BLK), t)
             before.append(jnp.where(behind, block.T, block))
         column = jnp.concatenate(
@@ -368,7 +410,7 @@
     rows_all, cross, panel, solved = pl.pallas_call(
         kernel,
         out_shape=(
-            jax.ShapeDtypeStruct((GRP, BLK, QUART, BLK), F32),
+            jax.ShapeDtypeStruct((GRP, TILE, NBLK, BLK), F32),
             jax.ShapeDtypeStruct((2, 4, 4, 2, BLK, BLK), F32),
             jax.ShapeDtypeStruct((BLK, 2 * BLK), F32),
             jax.ShapeDtypeStruct((BLK, 2 * BLK), F32),
@@ -382,14 +424,17 @@
             pltpu.VMEM((DEV, PIECE1, BLK), F32),
             pltpu.VMEM((DEV, PIECE1, BLK), F32),
             pltpu.VMEM((DEPTH, 2 * BLK), BF16),
-            pltpu.VMEM((NBLK * NBLK, BLK), F32),
-            pltpu.VMEM((DEV, PIECE2, BLK), F32),
-            pltpu.VMEM((DEV, PIECE2, BLK), F32),
+            pltpu.VMEM((TILE, 8, BLK), F32),
+            pltpu.VMEM((TILE, 8, BLK), F32),
+            pltpu.VMEM((TILE, NBLK, BLK), F32),
+            pltpu.VMEM((TILE, NBLK, BLK), F32),
+            pltpu.VMEM((5, BLK, BLK), F32),
             pltpu.VMEM((2, BLK, BLK), F32),
             pltpu.VMEM((BLK, BLK), F32),
             pltpu.VMEM((2, BLK, BLK), F32),
-            dma((STRIPS,)), dma((STRIPS,)), dma((2,)), dma((2,)), dma((5,)),
+            dma((STRIPS,)), dma((STRIPS,)), dma((5,)), dma((5,)), dma((6,)),
             dma((30,)), dma((30,)), dma((8,)), dma((8,)),
+            pltpu.SemaphoreType.REGULAR((3,)),
         ],
         compiler_params=pltpu.CompilerParams(
             collective_id=0, has_side_effects=True, vmem_limit_bytes=60 * 2**20),
@@ -404,7 +449,7 @@
             jax.ShapeDtypeStruct((BLK, NBLK * BLK), F32),
         ),
         in_specs=[
-            pl.BlockSpec((1, BLK, QUART, BLK), lambda n: (n, 0, 0, 0)),
+            pl.BlockSpec((GRP, TILE, QUART, BLK), lambda n: (0, 0, n, 0)),
             pl.BlockSpec((2, QUART, BLK, BLK), lambda n: (0, n, 0, 0)),
             small, small,
         ],

time: 86.1 us -> 74.6 us (0.87)
  Pallas kernels: 84.5 us -> 73.1 us
    pallas_call x1, Pallas kernels: 78.1 us -> 66.6 us  [on_device(): pl.pallas_call(kernel, out_shape=(jax.ShapeDtypeStruct((GRP, TILE, NBLK,...]
where the time goes in v3:
time: 74.6 us; the launch traced here: 74.4 us
  Pallas kernels  73.1 us (98%)
  between operations  1.28 us (2%)
    pallas_call x1, Pallas kernels, on_device(): pl.pallas_call(kernel, out_shape=(jax.ShapeDtypeStruct((GRP, TILE, NBLK,...  66.6 us
    pallas_call x1, Pallas kernels, on_device(): pl.pallas_call(update, grid=(GRP,), out_shape=(jax.ShapeDtypeStruct((BLK,...  6.48 us

profile of v3, /device:TPU:0, one launch (start us, length us, event | category | flops | bytes accessed | tf_op | source)
XLA Modules:
  0.0 74.4 jit_solution(15497580480935207603)
XLA Ops:
  1.3 66.6 %schur.1 = (f32[4,32,32,128]{3,2,1,0:T(8,128)}, f32[2,4,4,2,128,128]{5,4,3,2,1,0:T(8,128)}, f32[128,256]{1,0:T(8,128)}, f32[128,256]{1,0:T(8,128)}) custom-call(bf16[1,2560,2560]{2,1,0:T(8,128)(2,1)} %w_ref.1, bf16[1,2560,512]{2,1,0:T(8,128)(2,1)} %b_ref.1, f32[1,128]{1,0:T(1,128)} %bitcast.3, s32[1,4]{1,0:T(1,128)} %ids_ref.1, s32[1]{0:T(128)S(6)} %copy.7.count_ref), custom_call_target="tpu_custom_call" | custom-call | tf_op jit(solution)/shard_map/schur/pallas_call | solution.py:410
  67.9 6.5 %update.1 = (f32[128,256]{1,0:T(8,128)}, f32[128,4096]{1,0:T(8,128)}) custom-call(f32[4,32,32,128]{3,2,1,0:T(8,128)} %get-tuple-element.6.rows_ref, f32[2,32,128,128]{3,2,1,0:T(8,128)} %bitcast.2, f32[128,256]{1,0:T(8,128)} %get-tuple-element.8.panel_ref, f32[128,256]{1,0:T(8,128)} %get-tuple-element.9.solved_ref), custom_call_target="tpu_custom_call" | custom-call | tf_op jit(solution)/shard_map/update/pallas_call | solution.py:444

commit v4 on v3

--- a/solution.py
+++ b/solution.py
@@ -96,6 +96,7 @@
 def factor_steps(a_ref, v_ref, first, last):
     sub = iota((8, BLK), 0)
     lane = iota((8, BLK), 1)
+    left = first * 8
 
     def step(s, carry):
         base = pl.multiple_of(s * 8, 8)
@@ -115,15 +116,15 @@
             inv_rows = inv_rows - by * inv_rows[p:p + 1, :]
             for q in range(p + 1, 8):
                 cols[q] = cols[q] - by * cols[q][p:p + 1, :]
-        by = jnp.where(lane >= base + 8, rows * scale, 0.0).T
-        a = a_ref[...]
-        v = v_ref[...]
+        by = jnp.where(lane >= base + 8, rows * scale, 0.0).T[left:, :]
+        a = a_ref[left:, :]
+        v = v_ref[left:, :]
         for p in range(8):
-            column = jnp.broadcast_to(by[:, p:p + 1], (BLK, BLK))
+            column = jnp.broadcast_to(by[:, p:p + 1], (BLK - left, BLK))
             a = a - column * rows[p:p + 1, :]
             v = v - column * inv_rows[p:p + 1, :]
-        a_ref[...] = a
-        v_ref[...] = v
+        a_ref[left:, :] = a
+        v_ref[left:, :] = v
         v_ref[pl.ds(base, 8), :] = inv_rows * jnp.sqrt(scale)
         return carry
 
@@ -133,7 +134,7 @@
 def kernel(
     w_ref, b_ref, diag_ref, ids_ref, count_ref, rows_all, cross, panel_ref, solved_ref,
     wbuf, bbuf, gram, send1, recv1, rhs, send2, recv2, send3, recv3, small, mine, pivot, inverse,
-    wsem, bsem, send_sem, recv_sem, own_sem, ring_send, ring_recv, core_send, core_recv, greet_sem,
+    wsem, bsem, send_sem, recv_sem, own_sem, ring_send, ring_recv, core_send, core_recv, greet_sem, first_send, first_recv,
 ):
     g = lax.axis_index("grp")
     t = lax.axis_index("tile")
@@ -225,8 +226,33 @@
         exchanged[0].wait()
         exchanged[1].wait_recv()
 
-    sent1 = exchange(send1, recv1, pl.ds(0, SENT1), DEV, 0)
-    received(sent1)
+    sent_rows = pl.ds(0, SENT1)
+    sent1, planes = [], []
+    for dy in (2, 1, 3, 0):
+        def go1(k, carry, last=(dy + 1) * TILE - 1, first=dy * TILE + (0 if dy else 1)):
+            g2, t2 = peer_of(last + first - k, g, t)
+            pltpu.make_async_remote_copy(
+                send1.at[g2 * TILE + t2, sent_rows], recv1.at[me, sent_rows], first_send.at[dy],
+                first_recv.at[dy], device_id=(g2, t2), device_id_type=MESH).start()
+            return carry
+
+        first = 0 if dy else 1
+        lax.fori_loop(dy * TILE + first, (dy + 1) * TILE, go1, 0)
+        slab = recv1.at[pl.ds((g + 4 - dy) % 4 * TILE, TILE - first), sent_rows]
+        planes.append(dy)
+        sent1.append(pltpu.make_async_remote_copy(
+            slab, slab, first_send.at[dy], first_recv.at[dy], device_id=(g, t), device_id_type=MESH))
+    own_piece = pltpu.make_async_copy(send1.at[me, sent_rows], recv1.at[me, sent_rows], own_sem.at[0])
+    own_piece.start()
+    own_piece.wait()
+    used = iota((TILE, PIECE1, BLK), 1) < PAIRS
+    for made, dy in zip(sent1, planes):
+        made.wait_recv()
+        base = pl.multiple_of((g + 4 - dy) % 4 * TILE, TILE)
+        high, low = split(jnp.where(used, recv1[pl.ds(base, TILE)], 0.0).reshape(TILE * PIECE1, BLK))
+        place_rows = pl.ds(pl.multiple_of(base * PIECE1, TILE * PIECE1), TILE * PIECE1)
+        rhs[place_rows, 0:BLK] = high
+        rhs[place_rows, BLK:2 * BLK] = low
 
     extras = recv1[:, PAIRS, :]
     sel = iota((BLK, BLK), 0)
@@ -247,17 +273,12 @@
     own_row = iota((1, BLK), 1)
     own_key = jnp.where(own_row < NBLK, own_row * (NBLK + 1), -1)
     diag = jnp.where((lane == me) & (sel < NBLK), jnp.broadcast_to(extras[:, MAXB:MAXB + 1], (BLK, BLK)), 0.0)
-    used = iota((DEV, PIECE1, BLK), 1) < PAIRS
-    high, low = split(jnp.where(used, recv1[...], 0.0).reshape(PLACED, BLK))
-    rhs[0:PLACED, 0:BLK] = high
-    rhs[0:PLACED, BLK:2 * BLK] = low
     high, low = split(diag)
     rhs[PLACED:DEPTH, 0:BLK] = high
     rhs[PLACED:DEPTH, BLK:2 * BLK] = low
 
-    def place(m, carry):
-        base = pl.multiple_of(m * 256, 256)
-        place_row = iota((256, BLK), 0) + base
+    def placed(base, count):
+        place_row = iota((count, BLK), 0) + base
         row, col = place_row // NBLK, place_row % NBLK
         target = jnp.minimum(row, col) * NBLK + jnp.maximum(row, col)
         hot = [
@@ -265,51 +286,78 @@
         ]
         hot.append(jnp.where(target == own_key, F32(1), F32(0)).astype(BF16))
         both = dot(jnp.concatenate(hot, axis=1), rhs[...])
-        send3[pl.ds(m * 8, 8), :, :] = (both[:, 0:BLK] + both[:, BLK:2 * BLK]).reshape(8, NBLK, BLK)
-        return carry
-
-    lax.fori_loop(0, NBLK * NBLK // 256, place, 0)
-
+        return (both[:, 0:BLK] + both[:, BLK:2 * BLK]).reshape(count // NBLK, NBLK, BLK)
+
+    top = placed(0, 2 * NBLK)
     for b in range(2):
-        send2[:, b, :] = send3[b]
+        send2[:, b, :] = top[b]
     for e, (r, q) in enumerate(((0, 0), (0, 1), (1, 1))):
-        send2[:, 2 + e, :] = jnp.broadcast_to(send3[r, q:q + 1, :], (TILE, BLK))
+        send2[:, 2 + e, :] = jnp.broadcast_to(top[r, q:q + 1, :], (TILE, BLK))
     sent2 = exchange(send2, recv2, pl.ds(0, SENT2), TILE, 1)
-    sent3 = exchange(send3, recv3, pl.ds(0, NBLK), TILE, 2)
+
+    def send_rows(dx):
+        ahead, behind = (x + dx) % 4 * 8, (x + 4 - dx) % 4 * 8
+        send3[pl.ds(pl.multiple_of(ahead, 8), 8), :, :] = placed(ahead * NBLK, 8 * NBLK)
+
+        def go(k, carry):
+            t2 = ahead + (z + k // 2) % 4 * 2 + (c + k % 2) % 2
+            pltpu.make_async_remote_copy(
+                send3.at[t2], recv3.at[t], send_sem.at[2 + dx], recv_sem.at[2 + dx],
+                device_id=(g, t2), device_id_type=MESH).start()
+            return carry
+
+        first = 0 if dx else 1
+        lax.fori_loop(first, 8, go, 0)
+        slab = recv3.at[pl.ds(behind, 8 - first)]
+        return pltpu.make_async_remote_copy(
+            slab, slab, send_sem.at[2 + dx], recv_sem.at[2 + dx], device_id=(g, t), device_id_type=MESH)
+
+    sent3 = [send_rows(0)]
+    own_row = pltpu.make_async_copy(send3.at[t], recv3.at[t], own_sem.at[2])
+    own_row.start()
+    sent3.append(send_rows(1))
     received(sent2)
 
     part = pl.ds(pl.multiple_of(g * TILE, TILE), TILE)
     for e in range(5):
         small[e, part, :] = recv2[:, e, :]
     gathered = []
-    for slot, which in enumerate((pl.ds(2, 3), pl.ds(0, 2))):
+    for slot, which in enumerate((pl.ds(0, 2), pl.ds(2, 3))):
         for peer in (along_y[0], along_y[2], along_y[1]):
             pltpu.make_async_remote_copy(
-                small.at[which, part], small.at[which, part], send_sem.at[3 + slot], recv_sem.at[3 + slot],
+                small.at[which, part], small.at[which, part], send_sem.at[6 + slot], recv_sem.at[6 + slot],
                 device_id=peer, device_id_type=MESH).start()
         three = small.at[which, pl.ds(0, 3 * TILE)]
         gathered.append(pltpu.make_async_remote_copy(
-            three, three, send_sem.at[3 + slot], recv_sem.at[3 + slot], device_id=(g, t), device_id_type=MESH))
-
-    half, some = BLK // 2, TILE // 2
+            three, three, send_sem.at[6 + slot], recv_sem.at[6 + slot], device_id=(g, t), device_id_type=MESH))
+
+    half = BLK // 2
     side = lambda s: pl.ds(s * half, half)
-    row_side = lambda s: pl.ds(s * some, some)
     at_x = lambda i: (g, i * 8 + z * 2 + c)
     at_z = lambda i: (g, x * 8 + i * 2 + c)
     up, down = (lambda i: (i + 1) % 4), (lambda i: (i + 3) % 4)
-    ring_y = Ring(
-        lambda i, s: rows_all.at[i, row_side(s)], lambda s: recv3.at[row_side(s)], g,
-        (up(g), t), (down(g), t), ring_send, ring_recv, 0)
+    def ring_rows(slot, dx):
+        base = (x + 4 - dx) % 4 * 8
+        rows = lambda s: pl.ds(base + s * 4, 4)
+        return Ring(
+            lambda i, s: rows_all.at[i, rows(s)], lambda s: recv3.at[rows(s)], g,
+            (up(g), t), (down(g), t), ring_send, ring_recv, 24 + 6 * slot)
+
+    ring_y = [ring_rows(slot, dx) for slot, dx in enumerate((0, 1, 3, 2))]
+
+    def start_y(slot):
+        sent3[slot].wait_recv()
+        ring_y[slot].start()
 
     def ring(view, own, position, at, first):
         return Ring(view, own, position, at(up(position)), at(down(position)), ring_send, ring_recv, first)
 
     slab_a = lambda i, s: cross.at[0, :, i, c, side(s)]
     slab_b = lambda i, s: cross.at[1, i, :, c, side(s)]
-    ring_a1 = ring(lambda i, s: cross.at[0, i, z, c, side(s)], lambda s: mine.at[0, side(s)], x, at_x, 6)
-    ring_b1 = ring(lambda i, s: cross.at[1, x, i, c, side(s)], lambda s: mine.at[1, side(s)], z, at_z, 12)
-    ring_a2 = ring(slab_a, lambda s: slab_a(z, s), z, at_z, 18)
-    ring_b2 = ring(slab_b, lambda s: slab_b(x, s), x, at_x, 24)
+    ring_a1 = ring(lambda i, s: cross.at[0, i, z, c, side(s)], lambda s: mine.at[0, side(s)], x, at_x, 0)
+    ring_b1 = ring(lambda i, s: cross.at[1, x, i, c, side(s)], lambda s: mine.at[1, side(s)], z, at_z, 6)
+    ring_a2 = ring(slab_a, lambda s: slab_a(z, s), z, at_z, 12)
+    ring_b2 = ring(slab_b, lambda s: slab_b(x, s), x, at_x, 18)
     swaps = []
 
     def swap(view):
@@ -322,25 +370,29 @@
     eye = jnp.where(sel == lane, F32(1), F32(0))
     inverse[0] = eye
     inverse[1] = eye
+    own_row.wait()
+    start_y(0)
+    sent3.append(send_rows(3))
+    start_y(1)
+    sent3.append(send_rows(2))
     gathered[0].wait_recv()
-    pivot[...] = small[2]
-    gathered[1].wait_recv()
     mine[0] = small[0]
     mine[1] = jnp.where(jnp.full((BLK, BLK), t) == 0, small[1].T, small[1])
     ring_a1.start()
     ring_b1.start()
-    owns = [pltpu.make_async_copy(recv3, rows_all.at[g], own_sem.at[3])]
+    owns = []
     for b in range(2):
         owns.append(pltpu.make_async_copy(mine.at[b], cross.at[b, x, z, c], own_sem.at[4 + b]))
         owns[-1].start()
-    factor_steps(pivot, inverse.at[0], 0, 4)
-    received(sent3)
-    ring_y.start()
-    owns[0].start()
+    gathered[1].wait_recv()
+    pivot[...] = small[2]
+    factor_steps(pivot, inverse.at[0], 0, 3)
     ring_a1.middle()
     ring_b1.middle()
-    factor_steps(pivot, inverse.at[0], 4, 9)
-    for own in owns[1:]:
+    start_y(2)
+    ring_y[0].middle()
+    factor_steps(pivot, inverse.at[0], 3, 7)
+    for own in owns:
         own.wait()
     for made in (ring_a1, ring_b1):
         made.near()
@@ -349,57 +401,71 @@
     ring_b2.start()
     swap(cross.at[0, :, z, c])
     swap(cross.at[1, x, :, c])
-    factor_steps(pivot, inverse.at[0], 9, 16)
-    ring_y.middle()
+    ring_y[1].middle()
+    start_y(3)
+    owns.append(pltpu.make_async_copy(recv3, rows_all.at[g], own_sem.at[3]))
+    owns[-1].start()
+    factor_steps(pivot, inverse.at[0], 7, 13)
+    ring_y[2].middle()
+    factor_steps(pivot, inverse.at[0], 13, 16)
+    ring_y[3].middle()
+    ring_a2.middle()
+    ring_b2.middle()
     below = dot_full(small[3], inverse[0], ((0,), (1,)))
     pivot[...] = small[4] - dot_full(below, below, ((1,), (1,)))
-    ring_a2.middle()
-    ring_b2.middle()
-    factor_steps(pivot, inverse.at[1], 0, 6)
+    mixed = dot_full(below, inverse[0])
+    factor_steps(pivot, inverse.at[1], 0, 5)
     ring_a2.near()
     ring_b2.near()
     for step in (1, 3):
         swap(cross.at[0, :, (z + step) % 4, c])
         swap(cross.at[1, (x + step) % 4, :, c])
-    factor_steps(pivot, inverse.at[1], 6, 11)
+    factor_steps(pivot, inverse.at[1], 5, 9)
     ring_a2.end()
     ring_b2.end()
     swap(cross.at[0, :, (z + 2) % 4, c])
     swap(cross.at[1, (x + 2) % 4, :, c])
-    factor_steps(pivot, inverse.at[1], 11, 16)
-    first, second = inverse[0], inverse[1]
-    mixed = -dot_full(second, dot_full(below, first))
+    factor_steps(pivot, inverse.at[1], 9, 16)
     inv = jnp.concatenate(
-        [jnp.concatenate([first, jnp.zeros((BLK, BLK), F32)], axis=1),
-         jnp.concatenate([mixed, second], axis=1)], axis=0)
+        [jnp.concatenate([inverse[0], jnp.zeros((BLK, BLK), F32)], axis=1),
+         jnp.concatenate([-dot_full(inverse[1], mixed), inverse[1]], axis=1)], axis=0)
     panel = dot_full(jnp.concatenate([mine[0], mine[1]], axis=0), inv, ((0,), (1,)))
     panel_ref[...] = jnp.where(
         (jnp.full((BLK, 2 * BLK), t) == 0) & (iota((BLK, 2 * BLK), 1) >= BLK), 0.0, panel)
     solved_ref[...] = dot_full(panel, inv)
 
-    owns[0].wait()
-    ring_y.near()
-    ring_y.end()
+    owns[-1].wait()
+    for made in ring_y:
+        made.near()
+        made.end()
     for made in swaps:
         made.wait()
-    for made in (sent1[1], sent2[1], sent3[1], *gathered):
+    for made in (*sent1, sent2[1], *sent3, *gathered):
         made.wait_send()
+
+
+def split3(value):
+    high, rest = value.astype(BF16), value - value.astype(BF16).astype(F32)
+    middle = rest.astype(BF16)
+    return high, middle, (rest - middle.astype(F32)).astype(BF16)
 
 
 def update(rows_ref, cross_ref, panel_ref, solved_ref, panel_out, reduced_out):
     t = lax.axis_index("tile")
     n = pl.program_id(0)
     panel_out[...] = panel_ref[...]
+    left = jnp.concatenate(split3(solved_ref[...]), axis=0)
     for q in range(0, QUART, 2):
         before = []
         for e in range(q, q + 2):
             block = rows_ref[:, :, e, :].reshape(BLK, BLK)
             behind = jnp.full((BLK, BLK), n * QUART + e) < jnp.full((BLK, BLK), t)
             before.append(jnp.where(behind, block.T, block))
-        column = jnp.concatenate(
-            [jnp.concatenate([cross_ref[b, q], cross_ref[b, q + 1]], axis=1) for b in range(2)], axis=0)
-        reduced_out[:, q * BLK:(q + 2) * BLK] = jnp.concatenate(before, axis=1) - dot_full(
-            solved_ref[...], column)
+        right = split3(jnp.concatenate(
+            [jnp.concatenate([cross_ref[b, q], cross_ref[b, q + 1]], axis=1) for b in range(2)], axis=0))
+        one, two, three = dot(left, right[0]), dot(left[0:2 * BLK], right[1]), dot(left[0:BLK], right[2])
+        change = one[0:BLK] + (one[BLK:2 * BLK] + two[0:BLK] + (one[2 * BLK:] + two[BLK:] + three))
+        reduced_out[:, q * BLK:(q + 2) * BLK] = jnp.concatenate(before, axis=1) - change
 
 
 def on_device(inverse_factor, border, border_blocks, border_count, first_diag):
@@ -432,9 +498,9 @@
             pltpu.VMEM((2, BLK, BLK), F32),
             pltpu.VMEM((BLK, BLK), F32),
             pltpu.VMEM((2, BLK, BLK), F32),
-            dma((STRIPS,)), dma((STRIPS,)), dma((5,)), dma((5,)), dma((6,)),
-            dma((30,)), dma((30,)), dma((8,)), dma((8,)),
-            pltpu.SemaphoreType.REGULAR((3,)),
+            dma((STRIPS,)), dma((STRIPS,)), dma((8,)), dma((8,)), dma((6,)),
+            dma((48,)), dma((48,)), dma((8,)), dma((8,)),
+            pltpu.SemaphoreType.REGULAR((3,)), dma((GRP,)), dma((GRP,)),
         ],
         compiler_params=pltpu.CompilerParams(
             collective_id=0, has_side_effects=True, vmem_limit_bytes=60 * 2**20),

time: 74.6 us -> 73.2 us (0.981)
  Pallas kernels: 73.1 us -> 71.8 us
    pallas_call x1, Pallas kernels: 66.6 us -> 65.7 us  [on_device(): pl.pallas_call(kernel, out_shape=(jax.ShapeDtypeStruct((GRP, TILE, NBLK,...]
where the time goes in v4:
time: 73.2 us; the launch traced here: 73 us
  Pallas kernels  71.8 us (98%)
  between operations  1.28 us (2%)
    pallas_call x1, Pallas kernels, on_device(): pl.pallas_call(kernel, out_shape=(jax.ShapeDtypeStruct((GRP, TILE, NBLK,...  65.7 us
    pallas_call x1, Pallas kernels, on_device(): pl.pallas_call(update, grid=(GRP,), out_shape=(jax.ShapeDtypeStruct((BLK,...  6.06 us

profile of v4, /device:TPU:0, one launch (start us, length us, event | category | flops | bytes accessed | tf_op | source)
XLA Modules:
  0.0 73.0 jit_solution(7684584240502224613)
XLA Ops:
  1.3 65.7 %schur.1 = (f32[4,32,32,128]{3,2,1,0:T(8,128)}, f32[2,4,4,2,128,128]{5,4,3,2,1,0:T(8,128)}, f32[128,256]{1,0:T(8,128)}, f32[128,256]{1,0:T(8,128)}) custom-call(bf16[1,2560,2560]{2,1,0:T(8,128)(2,1)} %w_ref.1, bf16[1,2560,512]{2,1,0:T(8,128)(2,1)} %b_ref.1, f32[1,128]{1,0:T(1,128)} %bitcast.3, s32[1,4]{1,0:T(1,128)} %ids_ref.1, s32[1]{0:T(128)S(6)} %copy.7.count_ref), custom_call_target="tpu_custom_call" | custom-call | tf_op jit(solution)/shard_map/schur/pallas_call | solution.py:476
  67.0 6.1 %update.1 = (f32[128,256]{1,0:T(8,128)}, f32[128,4096]{1,0:T(8,128)}) custom-call(f32[4,32,32,128]{3,2,1,0:T(8,128)} %get-tuple-element.6.rows_ref, f32[2,32,128,128]{3,2,1,0:T(8,128)} %bitcast.2, f32[128,256]{1,0:T(8,128)} %get-tuple-element.8.panel_ref, f32[128,256]{1,0:T(8,128)} %get-tuple-element.9.solved_ref), custom_call_target="tpu_custom_call" | custom-call | tf_op jit(solution)/shard_map/update/pallas_call | solution.py:510

commit v5 on v4

--- a/solution.py
+++ b/solution.py
@@ -384,14 +384,11 @@
     for b in range(2):
         owns.append(pltpu.make_async_copy(mine.at[b], cross.at[b, x, z, c], own_sem.at[4 + b]))
         owns[-1].start()
+    ring_a1.middle()
+    ring_b1.middle()
     gathered[1].wait_recv()
     pivot[...] = small[2]
     factor_steps(pivot, inverse.at[0], 0, 3)
-    ring_a1.middle()
-    ring_b1.middle()
-    start_y(2)
-    ring_y[0].middle()
-    factor_steps(pivot, inverse.at[0], 3, 7)
     for own in owns:
         own.wait()
     for made in (ring_a1, ring_b1):
@@ -401,8 +398,11 @@
     ring_b2.start()
     swap(cross.at[0, :, z, c])
     swap(cross.at[1, x, :, c])
+    start_y(2)
+    ring_y[0].middle()
+    start_y(3)
+    factor_steps(pivot, inverse.at[0], 3, 7)
     ring_y[1].middle()
-    start_y(3)
     owns.append(pltpu.make_async_copy(recv3, rows_all.at[g], own_sem.at[3]))
     owns[-1].start()
     factor_steps(pivot, inverse.at[0], 7, 13)

time: 73.2 us -> 75.4 us (1.030)
  Pallas kernels: 71.8 us -> 73.9 us
    pallas_call x1, Pallas kernels: 65.7 us -> 67.9 us  [on_device(): pl.pallas_call(kernel, out_shape=(jax.ShapeDtypeStruct((GRP, TILE, NBLK,...]
where the time goes in v5:
time: 75.4 us; the launch traced here: 75.2 us
  Pallas kernels  73.9 us (98%)
  between operations  1.28 us (2%)
    pallas_call x1, Pallas kernels, on_device(): pl.pallas_call(kernel, out_shape=(jax.ShapeDtypeStruct((GRP, TILE, NBLK,...  67.9 us
    pallas_call x1, Pallas kernels, on_device(): pl.pallas_call(update, grid=(GRP,), out_shape=(jax.ShapeDtypeStruct((BLK,...  6.07 us

profile of v5, /device:TPU:0, one launch (start us, length us, event | category | flops | bytes accessed | tf_op | source)
XLA Modules:
  0.0 75.2 jit_solution(14343766162652952243)
XLA Ops:
  1.3 67.9 %schur.1 = (f32[4,32,32,128]{3,2,1,0:T(8,128)}, f32[2,4,4,2,128,128]{5,4,3,2,1,0:T(8,128)}, f32[128,256]{1,0:T(8,128)}, f32[128,256]{1,0:T(8,128)}) custom-call(bf16[1,2560,2560]{2,1,0:T(8,128)(2,1)} %w_ref.1, bf16[1,2560,512]{2,1,0:T(8,128)(2,1)} %b_ref.1, f32[1,128]{1,0:T(1,128)} %bitcast.3, s32[1,4]{1,0:T(1,128)} %ids_ref.1, s32[1]{0:T(128)S(6)} %copy.7.count_ref), custom_call_target="tpu_custom_call" | custom-call | tf_op jit(solution)/shard_map/schur/pallas_call | solution.py:476
  69.2 6.1 %update.1 = (f32[128,256]{1,0:T(8,128)}, f32[128,4096]{1,0:T(8,128)}) custom-call(f32[4,32,32,128]{3,2,1,0:T(8,128)} %get-tuple-element.6.rows_ref, f32[2,32,128,128]{3,2,1,0:T(8,128)} %bitcast.2, f32[128,256]{1,0:T(8,128)} %get-tuple-element.8.panel_ref, f32[128,256]{1,0:T(8,128)} %get-tuple-element.9.solved_ref), custom_call_target="tpu_custom_call" | custom-call | tf_op jit(solution)/shard_map/update/pallas_call | solution.py:510
